TPU v7x, 256 devices: a whole 4x4x8 slice. The times are simulated.
256 devices in a mesh: vol: 16 (over z, y_lo), ctl: 16 (over x, y_hi, core).
Axes of the slice: x: 4, y: 4 (y_hi: 2, y_lo: 2; y = y_hi * 2 + y_lo), z: 8, core: 2. Of those that a mesh axis runs over, the one named last changes fastest.
Arguments:
- node_points: float32 [3, 16, 32768], P(None, 'vol', 'ctl'), may hold values from -0.6 to 0.6
- cotangent: float32 [3, 16, 32768], P(None, 'vol', 'ctl'), may hold values from -6 to 6
- ctl_points: float32 [3, 16, 256], P(None, 'ctl', 'vol'), may hold values from -0.6 to 0.6
- ctl_weights: float32 [3, 16, 256], P(None, 'ctl', 'vol'), may hold values from -6 to 6
- tile_mask: int32 [16, 256, 16, 2], P('vol', None, 'ctl'), may hold values 0 or 1
Outputs:
- node_grad: float32 [3, 16, 32768], P(None, 'vol', 'ctl')
- weight_grad: float32 [3, 16, 256], P(None, 'ctl', 'vol')
- control_grad: float32 [3, 16, 256], P(None, 'ctl', 'vol')
All inputs are finite; a program needn't handle non-finite values. No bound on the sum of `tile_mask` on one device may be relied on, other than what follows from the above.
Results may differ from a plain program's by a relative error of at most 0.0001.
Values sent between devices are 32-bit elements; how exact they have to be, the bound alone decides.
No kernel may reach another device: no remote copies, remote signals or barrier semaphores. Data moves between devices by JAX's collectives and lax.ppermute only.
A program may use at most 192 MiB of HBM per device.

v0:
```python
import math

import jax
import jax.numpy as jnp
from jax import lax
from jax.sharding import PartitionSpec as P

TILE = 128


def tile_gradients(nodes, cots, ctl, wts, tiles, tile, pairs):
    rows = nodes.shape[1]
    cols = ctl.shape[1]
    units = rows // tile
    wanted = max(1, pairs // (cols * tile))
    factor = max([d for d in range(1, min(units, wanted) + 1) if units % d == 0])
    block = factor * tile
    count = rows // block
    tcols = tiles.shape[1]
    node_blocks = nodes.reshape(3, count, block).transpose(1, 0, 2)
    cot_blocks = cots.reshape(3, count, block).transpose(1, 0, 2)
    tile_blocks = tiles.reshape(count, factor, tcols)

    def step(carry, items):
        acc_w, acc_y = carry
        xb, gb, tb = items
        diff = xb[:, :, None] - ctl[:, None, :]
        dist = jnp.sqrt(jnp.sum(diff * diff, axis=0))
        near = jnp.maximum(1.0 - dist, 0.0)
        maskf = jnp.broadcast_to(
            tb.astype(jnp.float32)[:, None, :, None], (factor, tile, tcols, tile)
        ).reshape(block, cols)
        near3 = near * near * near
        phi = maskf * near3 * near * (4.0 * dist + 1.0)
        align = (
            gb[0][:, None] * wts[0][None, :]
            + gb[1][:, None] * wts[1][None, :]
            + gb[2][:, None] * wts[2][None, :]
        )
        force = maskf * -20.0 * near3 * align
        pulled = force[None] * diff
        node_part = jnp.sum(pulled, axis=2)
        acc_w = acc_w + jnp.sum(phi[None] * gb[:, :, None], axis=1)
        acc_y = acc_y - jnp.sum(pulled, axis=1)
        return ((acc_w, acc_y), node_part)

    zeros = jnp.zeros((3, cols), jnp.float32)
    (acc_w, acc_y), parts = lax.scan(step, (zeros, zeros), (node_blocks, cot_blocks, tile_blocks))
    node_part = parts.transpose(1, 0, 2).reshape(3, rows)
    return (node_part, acc_w, acc_y)


def local(node_points, cotangent, ctl_points, ctl_weights, tile_mask):
    n_vol = lax.axis_size("vol")
    n_ctl = lax.axis_size("ctl")
    total_nodes = node_points.shape[2] * n_ctl * n_vol
    total_ctl = ctl_points.shape[2] * n_vol * n_ctl
    ctl_block, wts_block = (
        lax.all_gather(ctl_points, "vol", axis=2, tiled=True),
        lax.all_gather(ctl_weights, "vol", axis=2, tiled=True),
    )
    width = ctl_block.shape[2]
    nodes, cots = (
        lax.all_gather(node_points, "ctl", axis=2, tiled=True),
        lax.all_gather(cotangent, "ctl", axis=2, tiled=True),
    )
    rows = nodes.shape[2]
    tiles = tile_mask.reshape(rows // TILE, width // TILE)
    node_part, acc_w, acc_y = tile_gradients(
        nodes.reshape(3, rows),
        cots.reshape(3, rows),
        ctl_block.reshape(3, width),
        wts_block.reshape(3, width),
        tiles,
        TILE,
        524288,
    )
    node_grad = lax.psum_scatter(
        node_part.reshape(3, 1, rows), "ctl", scatter_dimension=2, tiled=True
    )
    weight_grad, control_grad = (
        lax.psum_scatter(acc_w.reshape(3, 1, width), "vol", scatter_dimension=2, tiled=True),
        lax.psum_scatter(acc_y.reshape(3, 1, width), "vol", scatter_dimension=2, tiled=True),
    )
    node_grad = node_grad * (1.0 / math.sqrt(total_ctl))
    weight_grad = weight_grad * (1.0 / math.sqrt(total_nodes))
    control_grad = control_grad * (1.0 / math.sqrt(total_nodes))
    return (node_grad, weight_grad, control_grad)


def solution(mesh):
    placed = (
        P(None, "vol", "ctl"),
        P(None, "vol", "ctl"),
        P(None, "ctl", "vol"),
        P(None, "ctl", "vol"),
        P("vol", None, "ctl", None),
    )
    return jax.shard_map(
        local,
        mesh=mesh,
        in_specs=placed,
        out_specs=(P(None, "vol", "ctl"), P(None, "ctl", "vol"), P(None, "ctl", "vol")),
        check_vma=False,
    )
```

profile of v0, /device:TPU:2, one launch (start us, length us, event | category | flops | bytes accessed | tf_op | source)
XLA Modules:
  0.0 542.3 jit_solution(15718961345148010081)
XLA Ops:
  9.5 37.1 %all_gather.15 = f32[3,1,256]{0,1,2:T(1,128)S(1)} all-gather(f32[3,1,16]{0,1,2:T(1,128)S(1)} %copy.28), channel_id=1, replica_groups=mesh['vol'=16,'ctl'=16] {'vol'}, dimensions={2}, use_global_device_ids=true | all-gather | bytes 3264 | tf_op jit(solution)/shard_map/all_gather | solution.py:60
  46.7 30.2 %all_gather.13 = f32[3,1,256]{0,1,2:T(1,128)S(1)} all-gather(f32[3,1,16]{0,1,2:T(1,128)S(1)} %copy.27), channel_id=1, replica_groups=mesh['vol'=16,'ctl'=16] {'vol'}, dimensions={2}, use_global_device_ids=true | all-gather | bytes 3264 | tf_op jit(solution)/shard_map/all_gather | solution.py:59
  77.0 23.1 %all_gather.12 = f32[3,1,32768]{2,1,0:T(1,128)S(1)} all-gather(f32[3,1,2048]{2,1,0:T(1,128)} %param.7), channel_id=1, replica_groups=mesh['vol'=16,'ctl'=16] {'ctl'}, dimensions={2}, use_global_device_ids=true | all-gather | bytes 417792 | tf_op jit(solution)/shard_map/all_gather | solution.py:64
  100.1 20.6 %all_gather.14 = f32[3,1,32768]{2,1,0:T(1,128)S(1)} all-gather(f32[3,1,2048]{2,1,0:T(1,128)} %param.8), channel_id=1, replica_groups=mesh['vol'=16,'ctl'=16] {'ctl'}, dimensions={2}, use_global_device_ids=true | all-gather | bytes 417792 | tf_op jit(solution)/shard_map/all_gather | solution.py:65
  120.7 1.1 reduce
  121.8 1.1 reduce.1
  123.4 106.7 %while.15 = (s32[]{:T(128)}, f32[3,256]{1,0:T(4,128)S(1)}, f32[3,256]{1,0:T(4,128)S(1)}, f32[16,3,2048]{2,1,0:T(4,128)S(1)}, s32[16,16,2]{1,0,2:T(8,128)S(1)}, /...) while((s32[]{:T(128)}, f32[3,256]{1,0:T(4,128)S(1)}, ...), condition=%wide.region_5.6_spmd.clone, body=%wide.region_0.5_spmd.clone.sunk | while | flops 22539808 | bytes 17301516 | solution.py:48
  124.4 1.1 fusion.14
  125.5 1.7 fusion.17
  127.2 1.0 multiply_reduce_fusion.2
  128.2 1.9 fusion.18
  131.0 1.1 fusion.14
  132.1 1.7 fusion.17
  134.8 1.9 fusion.18
  137.7 1.1 fusion.14
  138.8 1.7 fusion.17
  141.5 1.9 fusion.18
  144.4 1.1 fusion.14
  145.5 1.7 fusion.17
  148.2 1.9 fusion.18
  151.0 1.1 fusion.14
  152.1 1.7 fusion.17
  154.8 1.9 fusion.18
  157.7 1.1 fusion.14
  158.8 1.7 fusion.17
  161.5 1.9 fusion.18
  164.4 1.1 fusion.14
  165.5 1.7 fusion.17
  168.2 1.9 fusion.18
  171.0 1.1 fusion.14
  172.1 1.7 fusion.17
  174.8 1.9 fusion.18
  177.7 1.1 fusion.14
  178.8 1.7 fusion.17
  181.5 1.9 fusion.18
  184.4 1.1 fusion.14
  185.5 1.7 fusion.17
  188.2 1.9 fusion.18
  191.0 1.1 fusion.14
  192.1 1.7 fusion.17
  194.8 1.9 fusion.18
  197.7 1.1 fusion.14
  198.8 1.7 fusion.17
  201.5 1.9 fusion.18
  204.4 1.1 fusion.14
  205.5 1.7 fusion.17
  208.2 1.9 fusion.18
  211.0 1.1 fusion.14
  212.1 1.7 fusion.17
  214.8 1.9 fusion.18
  217.7 1.1 fusion.14
  218.8 1.7 fusion.17
  221.5 1.9 fusion.18
  224.3 1.1 fusion.14
  225.5 1.7 fusion.17
  228.2 1.9 fusion.18
  230.4 1.0 bitcast_reduce_fusion.1
  231.7 1.0 bitcast_reduce_fusion.2
  233.7 39.6 %copy.35 = f32[3,1,32768]{1,0,2:T(4,128)} copy(f32[3,1,32768]{2,1,0:T(1,128)S(1)} %reshape_reshape.15) | data formatting | bytes 786432
  273.2 62.5 %bitcast_reduce_fusion = f32[32768,3]{1,0:T(8,128)} fusion(f32[3,1,32768]{1,0,2:T(4,128)} %copy.35), kind=kLoop, calls=%fused_computation.23 | loop fusion | bytes 786432
  336.7 33.1 %reduce-scatter.12.cloned.1.call-done = f32[16,3]{1,0:T(8,128)} async-done(((f32[256,3]{1,0:T(8,128)}), f32[16,3]{1,0:T(8,128)}) %reduce-scatter.12.cloned.1.call-update) | async-done | bytes 208
  371.8 154.9 %reduce-scatter.10.cloned.1.call-done = f32[2048,3]{1,0:T(8,128)} async-done(((f32[32768,3]{1,0:T(8,128)}), f32[2048,3]{1,0:T(8,128)}) %reduce-scatter.10.cloned.1.call-update) | async-done | bytes 24592
  526.7 5.1 reshape_bitcast_fusion
  531.8 3.4 copy.36
  (284 shorter events, 36.4 us)
Async XLA Ops:
  7.2 328.7 %reduce-scatter.14.cloned.1.call-start = ((), (), s32[]{:S(2)}) async-start(), calls=%async_computation.5 | async-start | bytes 139264
  231.4 138.4 %reduce-scatter.12.cloned.1.call-start = ((), (), s32[]{:S(2)}) async-start(), calls=%async_computation.4 | async-start | bytes 139264
  232.7 294.0 %reduce-scatter.10.cloned.1.call-start = ((), (), s32[]{:S(2)}) async-start(), calls=%async_computation.3 | async-start | bytes 17825792
Sparse Core Ops, SparseCore 0:
  231.5 67.7 reduce-scatter.13
  301.9 67.8 reduce-scatter.11
  374.5 152.1 reduce-scatter.9
where the time goes:
time: 544 us; the launch traced here: 542 us
  waiting for transfers between devices  188 us (35%)
  local copies, waits for them, and re-layouts  132 us (24%)
  blocking collectives  111 us (20%)
  other arithmetic  95 us (17%)
  between operations  13.8 us (3%)
    unnamed x6, waiting for transfers between devices  188 us
    unnamed x16, local copies, waits for them, and re-layouts  116 us
    all_gather x1, blocking collectives, local(): lax.all_gather(ctl_weights, 'vol', axis=2, tiled=True)  37.1 us
    all_gather x1, blocking collectives, local(): lax.all_gather(ctl_points, 'vol', axis=2, tiled=True)  30.2 us
    reduce_sum x16, other arithmetic, step(): node_part = jnp.sum(pulled, axis=2)  30.1 us
    mul x16, other arithmetic, step(): force = maskf * -20.0 * near3 * align  27.1 us
    all_gather x1, blocking collectives, local(): lax.all_gather(node_points, 'ctl', axis=2, tiled=True)  23.1 us
    all_gather x1, blocking collectives, local(): lax.all_gather(cotangent, 'ctl', axis=2, tiled=True)  20.6 us
  transfers between devices with their start and end apart: 3, of which 2 were waited for; matrix products, arithmetic and copies ran while one was open for 20% of the time, Pallas kernels for 0%

commit v1 on v0

v1 whole, which is shorter than its diff:
```python
import functools
import math

import jax
import jax.numpy as jnp
from jax import lax
from jax.experimental import pallas as pl
from jax.experimental.pallas import tpu as pltpu
from jax.sharding import PartitionSpec as P

TILE = 128
GROUP = 4
NODE_BITS = (8, 2, 4, 1)
CTL_BITS = (1, 2, 4, 8)
f32 = jnp.float32


def offset(place):
    return sum(bit for k, bit in enumerate(NODE_BITS) if place >> k & 1)


def swap(value, axis, bit):
    return lax.ppermute(value, axis, [(i, i ^ bit) for i in range(lax.axis_size(axis))])


def list_kernel(where_ref, mask_ref, list_ref, count_ref, *, places, units):
    tiles = places * units
    mine = where_ref[0]
    for half in range(2):
        n = jnp.int32(0)
        column = half ^ where_ref[1]
        for place in range(places):
            row = (mine ^ offset(place)) * units

            def step(k, n, place=place, row=row, column=column, half=half):
                list_ref[half, n] = place * units + k
                return n + jnp.where(mask_ref[row + k, column] != 0, 1, 0)

            n = lax.fori_loop(0, units, step, n, unroll=True)
        for k in range(GROUP):
            list_ref[half, n + k] = tiles
        count_ref[half] = (n + GROUP - 1) // GROUP


def pair_kernel(count_ref, list_ref, nod_ref, ctl_ref, send_ref, keep_ref, csum_ref, node_ref, acc_ref, *, tiles):
    node_ref[...] = jnp.zeros_like(node_ref)
    acc_ref[...] = jnp.zeros_like(acc_ref)
    for half in range(2):

        def body(i, _, half=half):
            ts = [list_ref[half, i * GROUP + b] for b in range(GROUP)]
            xg = [[jnp.broadcast_to(nod_ref[k, pl.ds(t, 1), :], (8, TILE)) for k in range(6)] for t in ts]
            node_sum = [[None] * 3 for _ in range(GROUP)]
            for c in range(TILE // 8):
                rows = pl.ds(half * TILE + c * 8, 8)
                yw = [ctl_ref[k, rows, :] for k in range(6)]
                ctl_sum = [None] * 6
                for b in range(GROUP):
                    x = xg[b][:3]
                    g = xg[b][3:]
                    diff = [x[k] - yw[k] for k in range(3)]
                    square = diff[0] * diff[0] + diff[1] * diff[1] + diff[2] * diff[2]
                    square = jnp.maximum(square, 1e-30)
                    dist = square * lax.rsqrt(square)
                    near = jnp.maximum(1.0 - dist, 0.0)
                    near2 = near * near
                    phi = near2 * near2 * (dist + 0.25)
                    align = g[0] * yw[3] + g[1] * yw[4] + g[2] * yw[5]
                    force = near2 * near * align
                    for k in range(3):
                        pulled = force * diff[k]
                        pushed = phi * g[k]
                        node_sum[b][k] = pulled if c == 0 else node_sum[b][k] + pulled
                        ctl_sum[3 + k] = pulled if b == 0 else ctl_sum[3 + k] + pulled
                        ctl_sum[k] = pushed if b == 0 else ctl_sum[k] + pushed
                for k in range(6):
                    acc_ref[k, rows, :] += ctl_sum[k]
            for b in range(GROUP):
                for k in range(3):
                    node_ref[k, pl.ds(ts[b], 1), :] += jnp.sum(node_sum[b][k], axis=0, keepdims=True)
            return 0

        lax.fori_loop(0, count_ref[half], body, 0)
    keep_ref[...] = node_ref[:, : tiles // 2, :]
    send_ref[...] = node_ref[:, tiles // 2 : tiles, :]
    ones = jnp.ones((8, TILE), f32)
    for k in range(6):
        total = lax.dot_general(
            ones, acc_ref[k], (((1,), (1,)), ((), ())), precision=lax.Precision.HIGHEST, preferred_element_type=f32
        )
        csum_ref[pl.ds(k, 1), :] = total[:1]


def local(node_points, cotangent, ctl_points, ctl_weights, tile_mask):
    n_vol = lax.axis_size("vol")
    n_ctl = lax.axis_size("ctl")
    own = node_points.shape[2]
    units = own // TILE
    tiles = units * n_ctl
    part = ctl_points.shape[2]
    width = part * n_vol
    total_nodes = own * n_ctl * n_vol
    total_ctl = width * n_ctl
    where = jnp.stack([lax.axis_index("ctl"), lax.axis_index("vol") * part // TILE]).astype(jnp.int32)

    nod = jnp.concatenate([node_points, cotangent], axis=0).reshape(6, units, TILE)
    ctl = jnp.concatenate([ctl_points, ctl_weights], axis=0).reshape(6, part)
    for node_bit, ctl_bit in zip(NODE_BITS, CTL_BITS):
        nod_new = swap(nod, "ctl", node_bit)
        ctl_new = swap(ctl, "vol", ctl_bit)
        nod = jnp.concatenate([nod, nod_new], axis=1)
        ctl = jnp.concatenate([ctl, ctl_new], axis=1)

    vmem = pl.BlockSpec(memory_space=pltpu.VMEM)
    smem = pl.BlockSpec(memory_space=pltpu.SMEM)
    lists, counts = pl.pallas_call(
        functools.partial(list_kernel, places=n_ctl, units=units),
        out_shape=(jax.ShapeDtypeStruct((2, tiles + 8), jnp.int32), jax.ShapeDtypeStruct((2,), jnp.int32)),
        in_specs=[smem, smem],
        out_specs=(smem, smem),
        name="kept_tiles",
    )(where, tile_mask.reshape(tiles, 2))
    send, keep, csum = pl.pallas_call(
        functools.partial(pair_kernel, tiles=tiles),
        out_shape=(
            jax.ShapeDtypeStruct((3, tiles // 2, TILE), f32),
            jax.ShapeDtypeStruct((3, tiles // 2, TILE), f32),
            jax.ShapeDtypeStruct((6, width), f32),
        ),
        in_specs=[smem, smem, vmem, vmem],
        out_specs=(vmem, vmem, vmem),
        scratch_shapes=[pltpu.VMEM((3, tiles + 8, TILE), f32), pltpu.VMEM((6, width, TILE), f32)],
        compiler_params=pltpu.CompilerParams(vmem_limit_bytes=32 << 20),
        name="pairs",
    )(
        counts,
        lists,
        jnp.pad(nod, ((0, 0), (0, 8), (0, 0))),
        jnp.broadcast_to(ctl[:, :, None], (6, width, TILE)),
    )
    size, span = tiles // 2, width // 2
    csend, ckeep = csum[:, span:], csum[:, :span]
    for node_bit, ctl_bit in zip(NODE_BITS[::-1], CTL_BITS[::-1]):
        send = swap(send, "ctl", node_bit)
        csend = swap(csend, "vol", ctl_bit)
        size, span = size // 2, span // 2
        if size >= units:
            send, keep = keep[:, size:] + send[:, size:], keep[:, :size] + send[:, :size]
            csend, ckeep = ckeep[:, span:] + csend[:, span:], ckeep[:, :span] + csend[:, :span]
        else:
            keep, ckeep = keep + send, ckeep + csend
    node_grad = keep.reshape(3, 1, own) * (-20.0 / math.sqrt(total_ctl))
    weight_grad = ckeep[:3].reshape(3, 1, part) * (4.0 / math.sqrt(total_nodes))
    control_grad = ckeep[3:].reshape(3, 1, part) * (20.0 / math.sqrt(total_nodes))
    return (node_grad, weight_grad, control_grad)


def solution(mesh):
    nodes = P(None, "vol", "ctl")
    ctl = P(None, "ctl", "vol")
    return jax.shard_map(
        local,
        mesh=mesh,
        in_specs=(nodes, nodes, ctl, ctl, P("vol", None, "ctl", None)),
        out_specs=(nodes, ctl, ctl),
        check_vma=False,
    )
```

time: 544 us -> 101 us (0.19)
  waiting for transfers between devices: 188 us -> 22.6 us
  local copies, waits for them, and re-layouts: 132 us -> 3.54 us
  blocking collectives: 111 us -> 0 us
  other arithmetic: 95 us -> 2.59 us
  Pallas kernels: 0 us -> 44.1 us
  starting transfers between devices: 0.3 us -> 26.2 us
  between operations: 13.8 us -> 0.79 us
    unnamed x6 -> x0, waiting for transfers between devices: 188 us -> none
    unnamed x16 -> x17, local copies, waits for them, and re-layouts: 116 us -> 3.12 us
    all_gather x4 -> x0, blocking collectives: 111 us -> none  [the longest x1 37.1 us: local(): lax.all_gather(ctl_weights, 'vol', axis=2, tiled=True)]
    reduce_sum x48 -> x0, other arithmetic: 63.6 us -> none  [the longest x16 30.1 us: step(): node_part = jnp.sum(pulled, axis=2)]
    pallas_call x0 -> x2, Pallas kernels: none -> 44.1 us  [the longest x1 38.4 us: local(): pl.pallas_call(functools.partial(pair_kernel, tiles=tiles), out_shape=(ja...]
    mul x19 -> x2, other arithmetic: 28.9 us -> 0.62 us  [the longest x1 0.62 us: local(): node_grad = keep.reshape(3, 1, own) * (-20.0 / math.sqrt(total_ctl))]
    ppermute x0 -> x16, starting transfers between devices: none -> 26.2 us  [swap(): lax.ppermute(value, axis, [(i, i ^ bit) for i in range(lax.axis_size(axis...]
    ppermute x0 -> x16, waiting for transfers between devices: none -> 22.6 us  [swap(): lax.ppermute(value, axis, [(i, i ^ bit) for i in range(lax.axis_size(axis...]
  transfers between devices with their start and end apart: 3 -> 16, of which waited for: 2 -> 9; matrix products, arithmetic and copies ran while one was open for 20% -> 4% of each run, Pallas kernels for 0% -> 6%
where the time goes in v1:
time: 101 us; the launch traced here: 99.8 us
  Pallas kernels  44.1 us (44%)
  starting transfers between devices  26.2 us (26%)
  waiting for transfers between devices  22.6 us (22%)
  local copies, waits for them, and re-layouts  3.54 us (4%)
  other arithmetic  2.59 us (3%)
    pallas_call x1, Pallas kernels, local(): pl.pallas_call(functools.partial(pair_kernel, tiles=tiles), out_shape=(ja...  38.4 us
    ppermute x16, starting transfers between devices, swap(): lax.ppermute(value, axis, [(i, i ^ bit) for i in range(lax.axis_size(axis...  26.2 us
    ppermute x16, waiting for transfers between devices, swap(): lax.ppermute(value, axis, [(i, i ^ bit) for i in range(lax.axis_size(axis...  22.6 us
    pallas_call x1, Pallas kernels, local(): pl.pallas_call(functools.partial(list_kernel, places=n_ctl, units=units),...  5.66 us
    unnamed x17, local copies, waits for them, and re-layouts  3.12 us
  transfers between devices with their start and end apart: 16, of which 9 were waited for; matrix products, arithmetic and copies ran while one was open for 4% of the time, Pallas kernels for 6%

profile of v1, /device:TPU:2, one launch (start us, length us, event | category | flops | bytes accessed | tf_op | source)
XLA Modules:
  0.0 99.8 jit_solution(1443283868340715030)
XLA Ops:
  0.6 0.0 copy-start.3
  0.6 0.7 copy.15
  1.3 0.0 copy-done.3
  1.3 1.7 %collective-permute-start.4 = (f32[6,16]{1,0:T(8,128)S(1)}, f32[6,16]{1,0:T(8,128)S(1)}, u32[]{:S(2)}, u32[]{:S(2)}) collective-permute-start(f32[6,16]{1,0:T(8,128)S(1)} %maximum_bitcast_fusion), channel_id=1, source_target_pairs={{0,16},{16,0},{32,48},{48,32},{64,80},{80,64},{96,112},{112,96},{1... | collective-permute-start | bytes 1160 | tf_op jit(solution)/shard_map/ppermute | solution.py:23
  3.0 0.8 pad_maximum_fusion.3
  3.8 2.2 %collective-permute-start = (f32[6,16,128]{2,1,0:T(8,128)S(1)}, f32[6,16,128]{2,1,0:T(8,128)S(1)}, u32[]{:S(2)}, u32[]{:S(2)}) collective-permute-start(f32[6,16,128]{2,1,0:T(8,128)S(1)} %bitcast.11), channel_id=1, source_target_pairs={{0,8},{1,9},{2,10},{3,11},{4,12},{5,13},{6,14},{7,15},{8,0},{9,1},... | collective-permute-start | bytes 147464 | tf_op jit(solution)/shard_map/ppermute | solution.py:23
  6.0 0.0 collective-permute-done.4
  6.0 0.1 pad_maximum_fusion.4
  6.1 1.9 %collective-permute-start.5 = (f32[6,32]{1,0:T(8,128)S(1)}, f32[6,32]{1,0:T(8,128)S(1)}, u32[]{:S(2)}, u32[]{:S(2)}) collective-permute-start(f32[6,32]{1,0:T(8,128)S(1)} %pad_maximum_fusion.4), channel_id=1, source_target_pairs={{0,32},{16,48},{32,0},{48,16},{64,96},{80,112},{96,64},{112,80},{1... | collective-permute-start | bytes 2312 | tf_op jit(solution)/shard_map/ppermute | solution.py:23
  8.0 1.5 %collective-permute-done = f32[6,16,128]{2,1,0:T(8,128)S(1)} collective-permute-done((f32[6,16,128]{2,1,0:T(8,128)S(1)}, f32[6,16,128]{2,1,0:T(8,128)S(1)}, u32[]{:S(2)}, u32[]{:S(2)}) %collective-permute-start) | collective-permute-done | bytes 49184 | tf_op jit(solution)/shard_map/ppermute | solution.py:23
  9.5 3.0 %collective-permute-start.1 = (f32[6,32,128]{2,1,0:T(8,128)S(1)}, f32[6,32,128]{2,1,0:T(8,128)S(1)}, u32[]{:S(2)}, u32[]{:S(2)}) collective-permute-start(f32[6,32,128]{2,1,0:T(8,128)S(1)} %pad_maximum_fusion.2), channel_id=1, source_target_pairs={{0,2},{1,3},{2,0},{3,1},{4,6},{5,7},{6,4},{7,5},{8,10},{9,11},{10,... | collective-permute-start | bytes 294920 | tf_op jit(solution)/shard_map/ppermute | solution.py:23
  12.5 0.0 collective-permute-done.5
  12.5 0.1 pad_maximum_fusion.5
  12.6 3.3 %collective-permute-start.6 = (f32[6,64]{1,0:T(8,128)S(1)}, f32[6,64]{1,0:T(8,128)S(1)}, u32[]{:S(2)}, u32[]{:S(2)}) collective-permute-start(f32[6,64]{1,0:T(8,128)S(1)} %pad_maximum_fusion.5), channel_id=1, source_target_pairs={{0,64},{16,80},{32,96},{48,112},{64,0},{80,16},{96,32},{112,48},{1... | collective-permute-start | bytes 4616 | tf_op jit(solution)/shard_map/ppermute | solution.py:23
  15.9 0.0 collective-permute-done.1
  15.9 0.6 collective-permute-start.2
  16.5 0.9 collective-permute-done.6
  17.5 0.1 pad_maximum_fusion.6
  17.5 6.9 %collective-permute-start.7 = (f32[6,128]{1,0:T(8,128)S(1)}, f32[6,128]{1,0:T(8,128)S(1)}, u32[]{:S(2)}, u32[]{:S(2)}) collective-permute-start(f32[6,128]{1,0:T(8,128)S(1)} %pad_maximum_fusion.6), channel_id=1, source_target_pairs={{0,128},{16,144},{32,160},{48,176},{64,192},{80,208},{96,224},{112... | collective-permute-start | bytes 9224 | tf_op jit(solution)/shard_map/ppermute | solution.py:23
  24.4 0.0 collective-permute-done.2
  24.4 0.1 collective-permute-start.3
  24.5 0.0 copy-start.2
  24.5 0.6 pad_add_fusion.where_ref
  25.2 0.1 copy-done.2
  25.2 0.8 copy.14
  26.0 5.7 %kept_tiles.1 = (s32[2,264]{1,0:T(2,128)}, s32[2]{0:T(128)}) custom-call(s32[2]{0:T(128)} %pad_add_fusion.where_ref, s32[256,2]{1,0:T(8,128)} %bitcast.16), custom_call_target="tpu_custom_call" | custom-call | tf_op jit(solution)/shard_map/kept_tiles/pallas_call | solution.py:116
  31.7 0.0 collective-permute-done.7
  31.7 0.1 concatenate.45
  31.8 0.0 collective-permute-done.3
  31.9 0.1 pad.4.nod_ref
  31.9 0.0 copy-start
  31.9 0.0 copy-start.1
  31.9 0.3 broadcast_in_dim.2.ctl_ref
  32.2 0.4 copy-done
  32.6 0.0 copy-done.1
  32.6 38.4 %pairs.1 = (f32[3,128,128]{2,1,0:T(8,128)S(1)}, f32[3,128,128]{2,1,0:T(8,128)S(1)}, f32[6,256]{1,0:T(8,128)S(1)}) custom-call(s32[2]{0:T(128)S(1)} %copy-done.1, s32[2,264]{1,0:T(2,128)S(1)} %copy-done, f32[6,264,128]{2,1,0:T(8,128)S(1)} %pad.4.nod_ref, f32[6,256,128]{2,1,0:T(8,128)S(1)} %broadcast_in_dim.2.ctl_ref), custom_call_target="tpu_custom_call" | custom-call | tf_op jit(solution)/shard_map/pairs/pallas_call | solution.py:123
  71.0 1.3 %collective-permute-start.12 = (f32[6,128]{1,0:T(8,128)S(1)}, f32[6,128]{1,0:T(8,128)S(1)}, u32[]{:S(2)}, u32[]{:S(2)}) collective-permute-start(f32[6,128]{1,0:T(8,128)S(1)} %slice.97), channel_id=1, source_target_pairs={{0,128},{16,144},{32,160},{48,176},{64,192},{80,208},{96,224},{112... | collective-permute-start | bytes 9224 | tf_op jit(solution)/shard_map/ppermute | solution.py:23
  72.4 6.2 %collective-permute-done.12 = f32[6,128]{1,0:T(8,128)S(1)} collective-permute-done((f32[6,128]{1,0:T(8,128)S(1)}, f32[6,128]{1,0:T(8,128)S(1)}, u32[]{:S(2)}, u32[]{:S(2)}) %collective-permute-start.12) | collective-permute-done | bytes 3104 | tf_op jit(solution)/shard_map/ppermute | solution.py:23
  78.6 0.1 slice_add_fusion.10
  78.6 0.0 collective-permute-start.13
  78.7 0.1 collective-permute-start.8
  78.8 4.4 %collective-permute-done.13 = f32[6,64]{1,0:T(8,128)S(1)} collective-permute-done((f32[6,64]{1,0:T(8,128)S(1)}, f32[6,64]{1,0:T(8,128)S(1)}, u32[]{:S(2)}, u32[]{:S(2)}) %collective-permute-start.13) | collective-permute-done | bytes 1568 | tf_op jit(solution)/shard_map/ppermute | solution.py:23
  83.2 0.1 slice_add_fusion.8
  83.2 0.1 collective-permute-start.14
  83.4 0.0 collective-permute-done.8
  83.4 0.7 collective-permute-start.9
  84.1 2.8 %collective-permute-done.14 = f32[6,32]{1,0:T(8,128)S(1)} collective-permute-done((f32[6,32]{1,0:T(8,128)S(1)}, f32[6,32]{1,0:T(8,128)S(1)}, u32[]{:S(2)}, u32[]{:S(2)}) %collective-permute-start.14) | collective-permute-done | bytes 800 | tf_op jit(solution)/shard_map/ppermute | solution.py:23
  86.9 0.1 slice_add_fusion.6
  86.9 0.0 collective-permute-start.15
  86.9 1.2 %collective-permute-done.9 = f32[3,64,128]{2,1,0:T(8,128)S(1)} collective-permute-done((f32[3,64,128]{2,1,0:T(8,128)S(1)}, f32[3,64,128]{2,1,0:T(8,128)S(1)}, u32[]{:S(2)}, u32[]{:S(2)}) %collective-permute-start.9) | collective-permute-done | bytes 98336 | tf_op jit(solution)/shard_map/ppermute | solution.py:23
  88.1 1.9 %collective-permute-start.10 = (f32[3,32,128]{2,1,0:T(8,128)S(1)}, f32[3,32,128]{2,1,0:T(8,128)S(1)}, u32[]{:S(2)}, u32[]{:S(2)}) collective-permute-start(f32[3,32,128]{2,1,0:T(8,128)S(1)} %get-tuple-element.22), channel_id=1, source_target_pairs={{0,2},{1,3},{2,0},{3,1},{4,6},{5,7},{6,4},{7,5},{8,10},{9,11},{10,... | collective-permute-start | bytes 147464 | tf_op jit(solution)/shard_map/ppermute | solution.py:23
  90.0 0.5 collective-permute-done.15
  90.6 3.2 %collective-permute-done.10 = f32[3,32,128]{2,1,0:T(8,128)S(1)} collective-permute-done((f32[3,32,128]{2,1,0:T(8,128)S(1)}, f32[3,32,128]{2,1,0:T(8,128)S(1)}, u32[]{:S(2)}, u32[]{:S(2)}) %collective-permute-start.10) | collective-permute-done | bytes 49184 | tf_op jit(solution)/shard_map/ppermute | solution.py:23
  93.8 2.3 %collective-permute-start.11 = (f32[3,16,128]{2,1,0:T(8,128)S(1)}, f32[3,16,128]{2,1,0:T(8,128)S(1)}, u32[]{:S(2)}, u32[]{:S(2)}) collective-permute-start(f32[3,16,128]{2,1,0:T(8,128)S(1)} %slice_add_fusion.4), channel_id=1, source_target_pairs={{0,8},{1,9},{2,10},{3,11},{4,12},{5,13},{6,14},{7,15},{8,0},{9,1},... | collective-permute-start | bytes 73736 | tf_op jit(solution)/shard_map/ppermute | solution.py:23
  96.1 0.6 copy.18
  96.7 0.6 copy.19
  97.3 1.9 %collective-permute-done.11 = f32[3,16,128]{2,1,0:T(8,128)S(1)} collective-permute-done((f32[3,16,128]{2,1,0:T(8,128)S(1)}, f32[3,16,128]{2,1,0:T(8,128)S(1)}, u32[]{:S(2)}, u32[]{:S(2)}) %collective-permute-start.11) | collective-permute-done | bytes 24608 | tf_op jit(solution)/shard_map/ppermute | solution.py:23
  99.1 0.6 fusion.1
  (16 shorter events, 0.2 us)
Async XLA Ops:
  0.6 0.7 copy-start.3
  1.3 4.7 %collective-permute-start.4 = (f32[6,16]{1,0:T(8,128)S(1)}, f32[6,16]{1,0:T(8,128)S(1)}, u32[]{:S(2)}, u32[]{:S(2)}) collective-permute-start(f32[6,16]{1,0:T(8,128)S(1)} %maximum_bitcast_fusion), channel_id=1, source_target_pairs={{0,16},{16,0},{32,48},{48,32},{64,80},{80,64},{96,112},{112,96},{1... | collective-permute-start | bytes 1160 | tf_op jit(solution)/shard_map/ppermute | solution.py:23
  3.8 5.7 %collective-permute-start = (f32[6,16,128]{2,1,0:T(8,128)S(1)}, f32[6,16,128]{2,1,0:T(8,128)S(1)}, u32[]{:S(2)}, u32[]{:S(2)}) collective-permute-start(f32[6,16,128]{2,1,0:T(8,128)S(1)} %bitcast.11), channel_id=1, source_target_pairs={{0,8},{1,9},{2,10},{3,11},{4,12},{5,13},{6,14},{7,15},{8,0},{9,1},... | collective-permute-start | bytes 147464 | tf_op jit(solution)/shard_map/ppermute | solution.py:23
  6.1 6.4 %collective-permute-start.5 = (f32[6,32]{1,0:T(8,128)S(1)}, f32[6,32]{1,0:T(8,128)S(1)}, u32[]{:S(2)}, u32[]{:S(2)}) collective-permute-start(f32[6,32]{1,0:T(8,128)S(1)} %pad_maximum_fusion.4), channel_id=1, source_target_pairs={{0,32},{16,48},{32,0},{48,16},{64,96},{80,112},{96,64},{112,80},{1... | collective-permute-start | bytes 2312 | tf_op jit(solution)/shard_map/ppermute | solution.py:23
  9.5 6.4 %collective-permute-start.1 = (f32[6,32,128]{2,1,0:T(8,128)S(1)}, f32[6,32,128]{2,1,0:T(8,128)S(1)}, u32[]{:S(2)}, u32[]{:S(2)}) collective-permute-start(f32[6,32,128]{2,1,0:T(8,128)S(1)} %pad_maximum_fusion.2), channel_id=1, source_target_pairs={{0,2},{1,3},{2,0},{3,1},{4,6},{5,7},{6,4},{7,5},{8,10},{9,11},{10,... | collective-permute-start | bytes 294920 | tf_op jit(solution)/shard_map/ppermute | solution.py:23
  12.6 4.9 %collective-permute-start.6 = (f32[6,64]{1,0:T(8,128)S(1)}, f32[6,64]{1,0:T(8,128)S(1)}, u32[]{:S(2)}, u32[]{:S(2)}) collective-permute-start(f32[6,64]{1,0:T(8,128)S(1)} %pad_maximum_fusion.5), channel_id=1, source_target_pairs={{0,64},{16,80},{32,96},{48,112},{64,0},{80,16},{96,32},{112,48},{1... | collective-permute-start | bytes 4616 | tf_op jit(solution)/shard_map/ppermute | solution.py:23
  15.9 8.5 %collective-permute-start.2 = (f32[6,64,128]{2,1,0:T(8,128)S(1)}, f32[6,64,128]{2,1,0:T(8,128)S(1)}, u32[]{:S(2)}, u32[]{:S(2)}) collective-permute-start(f32[6,64,128]{2,1,0:T(8,128)S(1)} %pad_maximum_fusion.1), channel_id=1, source_target_pairs={{0,4},{1,5},{2,6},{3,7},{4,0},{5,1},{6,2},{7,3},{8,12},{9,13},{10,... | collective-permute-start | bytes 589832 | tf_op jit(solution)/shard_map/ppermute | solution.py:23
  17.5 14.1 %collective-permute-start.7 = (f32[6,128]{1,0:T(8,128)S(1)}, f32[6,128]{1,0:T(8,128)S(1)}, u32[]{:S(2)}, u32[]{:S(2)}) collective-permute-start(f32[6,128]{1,0:T(8,128)S(1)} %pad_maximum_fusion.6), channel_id=1, source_target_pairs={{0,128},{16,144},{32,160},{48,176},{64,192},{80,208},{96,224},{112... | collective-permute-start | bytes 9224 | tf_op jit(solution)/shard_map/ppermute | solution.py:23
  24.4 7.4 %collective-permute-start.3 = (f32[6,128,128]{2,1,0:T(8,128)S(1)}, f32[6,128,128]{2,1,0:T(8,128)S(1)}, u32[]{:S(2)}, u32[]{:S(2)}) collective-permute-start(f32[6,128,128]{2,1,0:T(8,128)S(1)} %pad_maximum_fusion), channel_id=1, source_target_pairs={{0,1},{1,0},{2,3},{3,2},{4,5},{5,4},{6,7},{7,6},{8,9},{9,8},{10,11... | collective-permute-start | bytes 1179656 | tf_op jit(solution)/shard_map/ppermute | solution.py:23
  24.5 0.7 copy-start.2
  31.9 0.7 copy-start
  31.9 0.7 copy-start.1
  71.0 7.5 %collective-permute-start.12 = (f32[6,128]{1,0:T(8,128)S(1)}, f32[6,128]{1,0:T(8,128)S(1)}, u32[]{:S(2)}, u32[]{:S(2)}) collective-permute-start(f32[6,128]{1,0:T(8,128)S(1)} %slice.97), channel_id=1, source_target_pairs={{0,128},{16,144},{32,160},{48,176},{64,192},{80,208},{96,224},{112... | collective-permute-start | bytes 9224 | tf_op jit(solution)/shard_map/ppermute | solution.py:23
  78.6 4.5 %collective-permute-start.13 = (f32[6,64]{1,0:T(8,128)S(1)}, f32[6,64]{1,0:T(8,128)S(1)}, u32[]{:S(2)}, u32[]{:S(2)}) collective-permute-start(f32[6,64]{1,0:T(8,128)S(1)} %get-tuple-element.24), channel_id=1, source_target_pairs={{0,64},{16,80},{32,96},{48,112},{64,0},{80,16},{96,32},{112,48},{1... | collective-permute-start | bytes 4616 | tf_op jit(solution)/shard_map/ppermute | solution.py:23
  78.7 4.7 %collective-permute-start.8 = (f32[3,128,128]{2,1,0:T(8,128)S(1)}, f32[3,128,128]{2,1,0:T(8,128)S(1)}, u32[]{:S(2)}, u32[]{:S(2)}) collective-permute-start(f32[3,128,128]{2,1,0:T(8,128)S(1)} %get-tuple-element.11), channel_id=1, source_target_pairs={{0,1},{1,0},{2,3},{3,2},{4,5},{5,4},{6,7},{7,6},{8,9},{9,8},{10,11... | collective-permute-start | bytes 589832 | tf_op jit(solution)/shard_map/ppermute | solution.py:23
  83.2 3.6 %collective-permute-start.14 = (f32[6,32]{1,0:T(8,128)S(1)}, f32[6,32]{1,0:T(8,128)S(1)}, u32[]{:S(2)}, u32[]{:S(2)}) collective-permute-start(f32[6,32]{1,0:T(8,128)S(1)} %get-tuple-element.26), channel_id=1, source_target_pairs={{0,32},{16,48},{32,0},{48,16},{64,96},{80,112},{96,64},{112,80},{1... | collective-permute-start | bytes 2312 | tf_op jit(solution)/shard_map/ppermute | solution.py:23
  83.4 4.7 %collective-permute-start.9 = (f32[3,64,128]{2,1,0:T(8,128)S(1)}, f32[3,64,128]{2,1,0:T(8,128)S(1)}, u32[]{:S(2)}, u32[]{:S(2)}) collective-permute-start(f32[3,64,128]{2,1,0:T(8,128)S(1)} %get-tuple-element.20), channel_id=1, source_target_pairs={{0,4},{1,5},{2,6},{3,7},{4,0},{5,1},{6,2},{7,3},{8,12},{9,13},{10,... | collective-permute-start | bytes 294920 | tf_op jit(solution)/shard_map/ppermute | solution.py:23
  86.9 3.6 %collective-permute-start.15 = (f32[6,16]{1,0:T(8,128)S(1)}, f32[6,16]{1,0:T(8,128)S(1)}, u32[]{:S(2)}, u32[]{:S(2)}) collective-permute-start(f32[6,16]{1,0:T(8,128)S(1)} %slice_add_fusion.6), channel_id=1, source_target_pairs={{0,16},{16,0},{32,48},{48,32},{64,80},{80,64},{96,112},{112,96},{1... | collective-permute-start | bytes 1160 | tf_op jit(solution)/shard_map/ppermute | solution.py:23
  88.1 5.7 %collective-permute-start.10 = (f32[3,32,128]{2,1,0:T(8,128)S(1)}, f32[3,32,128]{2,1,0:T(8,128)S(1)}, u32[]{:S(2)}, u32[]{:S(2)}) collective-permute-start(f32[3,32,128]{2,1,0:T(8,128)S(1)} %get-tuple-element.22), channel_id=1, source_target_pairs={{0,2},{1,3},{2,0},{3,1},{4,6},{5,7},{6,4},{7,5},{8,10},{9,11},{10,... | collective-permute-start | bytes 147464 | tf_op jit(solution)/shard_map/ppermute | solution.py:23
  93.8 5.3 %collective-permute-start.11 = (f32[3,16,128]{2,1,0:T(8,128)S(1)}, f32[3,16,128]{2,1,0:T(8,128)S(1)}, u32[]{:S(2)}, u32[]{:S(2)}) collective-permute-start(f32[3,16,128]{2,1,0:T(8,128)S(1)} %slice_add_fusion.4), channel_id=1, source_target_pairs={{0,8},{1,9},{2,10},{3,11},{4,12},{5,13},{6,14},{7,15},{8,0},{9,1},... | collective-permute-start | bytes 73736 | tf_op jit(solution)/shard_map/ppermute | solution.py:23

commit v2 on v1

v2 whole, which is shorter than its diff:
```python
import functools
import math

import jax
import jax.numpy as jnp
from jax import lax
from jax.experimental import pallas as pl
from jax.experimental.pallas import tpu as pltpu
from jax.sharding import PartitionSpec as P

TILE = 128
GROUP = 4
SHIFT = 1024
NODE_BITS = (12, 2, 4, 1)
CTL_BITS = (12, 4, 2, 1)
SUM_BITS = (12, 2, 4, 1)
CALLS = ((8, 8), (0, 8))
f32 = jnp.float32


def xor_of(bits, index):
    return functools.reduce(lambda a, b: a ^ b, [bit for k, bit in enumerate(bits) if index >> k & 1], 0)


def offset(slot):
    return xor_of(SUM_BITS[::-1], slot)


def place(slot):
    return [xor_of(NODE_BITS, p) for p in range(1 << len(NODE_BITS))].index(offset(slot))


def swap(value, axis, bit):
    return lax.ppermute(value, axis, [(i, i ^ bit) for i in range(lax.axis_size(axis))])


def list_kernel(where_ref, mask_ref, list_ref, count_ref, *, units, stride):
    lists = [(call, half) for call in range(len(CALLS)) for half in range(2)]
    found = [jnp.int32(j * stride) for j in range(len(lists))]
    columns = [half ^ where_ref[1] for half in range(2)]
    for i in range(max(blocks for _, blocks in CALLS)):
        live = [j for j, (call, _) in enumerate(lists) if i < CALLS[call][1]]
        rows = {}
        for j in live:
            call, half = lists[j]
            rows[j] = (where_ref[0] ^ offset(CALLS[call][0] + i)) * (2 * units) + columns[half]
        for k in range(units):
            for j in live:
                call, half = lists[j]
                list_ref[found[j]] = (place(CALLS[call][0] + i) * units + k) * SHIFT + i * units + k
                found[j] = found[j] + mask_ref[rows[j] + 2 * k]
    for j, (call, half) in enumerate(lists):
        for k in range(GROUP):
            list_ref[found[j] + k] = (units << len(NODE_BITS)) * SHIFT + CALLS[call][1] * units
        count_ref[j] = (found[j] - j * stride + GROUP - 1) // GROUP


def pair_kernel(count_ref, list_ref, nod_ref, ctl_ref, before_ref, part_ref, csum_ref, node_ref, acc_ref, *, call, stride, part):
    node_ref[...] = jnp.zeros_like(node_ref)
    acc_ref[...] = jnp.zeros_like(acc_ref)
    for half in range(2):
        row = 2 * call + half
        starts = [s for s in range(0, acc_ref.shape[1], 8) if s // part % 2 == half]

        def body(i, _, row=row, starts=starts):
            items = [list_ref[row * stride + i * GROUP + b] for b in range(GROUP)]
            ts = [item >> 10 for item in items]
            outs = [item & (SHIFT - 1) for item in items]
            xg = [[jnp.broadcast_to(nod_ref[k, pl.ds(t, 1), :], (8, TILE)) for k in range(6)] for t in ts]
            node_sum = [[None] * 3 for _ in range(GROUP)]
            for c, start in enumerate(starts):
                rows = pl.ds(start, 8)
                yw = [ctl_ref[k, rows, :] for k in range(6)]
                ctl_sum = [None] * 6
                for b in range(GROUP):
                    x = xg[b][:3]
                    g = xg[b][3:]
                    diff = [x[k] - yw[k] for k in range(3)]
                    square = diff[0] * diff[0] + diff[1] * diff[1] + diff[2] * diff[2]
                    dist = pl.reciprocal(lax.rsqrt(square), approx=True)
                    near = jnp.maximum(1.0 - dist, 0.0)
                    near2 = near * near
                    phi = near2 * near2 * (dist + 0.25)
                    align = g[0] * yw[3] + g[1] * yw[4] + g[2] * yw[5]
                    force = near2 * near * align
                    for k in range(3):
                        pulled = force * diff[k]
                        pushed = phi * g[k]
                        node_sum[b][k] = pulled if c == 0 else node_sum[b][k] + pulled
                        ctl_sum[3 + k] = pulled if b == 0 else ctl_sum[3 + k] + pulled
                        ctl_sum[k] = pushed if b == 0 else ctl_sum[k] + pushed
                for k in range(6):
                    acc_ref[k, rows, :] += ctl_sum[k]
            for b in range(GROUP):
                for k in range(3):
                    node_ref[k, pl.ds(outs[b], 1), :] += jnp.sum(node_sum[b][k], axis=0, keepdims=True)
            return 0

        lax.fori_loop(0, count_ref[row], body, 0)
    part_ref[...] = node_ref[:, : part_ref.shape[1], :]
    for k in range(6):
        for s in range(0, acc_ref.shape[1], TILE):
            total = jnp.sum(acc_ref[k, pl.ds(s, TILE), :].T, axis=0, keepdims=True)
            csum_ref[pl.ds(k, 1), pl.ds(s, TILE)] = before_ref[pl.ds(k, 1), pl.ds(s, TILE)] + total


def local(node_points, cotangent, ctl_points, ctl_weights, tile_mask):
    n_vol = lax.axis_size("vol")
    n_ctl = lax.axis_size("ctl")
    own = node_points.shape[2]
    units = own // TILE
    tiles = units * n_ctl
    part = ctl_points.shape[2]
    width = part * n_vol
    total_nodes = own * n_ctl * n_vol
    total_ctl = width * n_ctl
    vmem = pl.BlockSpec(memory_space=pltpu.VMEM)
    smem = pl.BlockSpec(memory_space=pltpu.SMEM)
    stride = max(blocks for _, blocks in CALLS) * units + 8
    where = jnp.stack([lax.axis_index("ctl"), lax.axis_index("vol") * part // TILE]).astype(jnp.int32)
    mask = tile_mask.reshape(2 * tiles)

    nod = jnp.concatenate([node_points, cotangent], axis=0).reshape(6, units, TILE)
    ctl = jnp.concatenate([ctl_points, ctl_weights], axis=0).reshape(6, part)
    for step, (node_bit, ctl_bit) in enumerate(zip(NODE_BITS, CTL_BITS)):
        nod_new = swap(nod, "ctl", node_bit)
        ctl_new = swap(ctl, "vol", ctl_bit)
        if step == 1:
            nod_new, where, mask = lax.optimization_barrier((nod_new, where, mask))
        if step == 2:
            lists, counts = pl.pallas_call(
                functools.partial(list_kernel, units=units, stride=stride),
                out_shape=(
                    jax.ShapeDtypeStruct((2 * len(CALLS) * stride,), jnp.int32),
                    jax.ShapeDtypeStruct((2 * len(CALLS),), jnp.int32),
                ),
                in_specs=[smem, smem],
                out_specs=(smem, smem),
                name="kept_tiles",
            )(where, mask)
            nod_new, lists, counts = lax.optimization_barrier((nod_new, lists, counts))
        nod = jnp.concatenate([nod, nod_new], axis=1)
        ctl = jnp.concatenate([ctl, ctl_new], axis=1)
    nod = jnp.pad(nod, ((0, 0), (0, 8), (0, 0)))
    ctl = jnp.broadcast_to(ctl[:, :, None], (6, width, TILE))

    def pairs(call, csum):
        rows = CALLS[call][1] * units
        work = rows * TILE * width
        return pl.pallas_call(
            functools.partial(pair_kernel, call=call, stride=stride, part=part),
            out_shape=(jax.ShapeDtypeStruct((3, rows, TILE), f32), jax.ShapeDtypeStruct((6, width), f32)),
            in_specs=[smem, smem, vmem, vmem, vmem],
            out_specs=(vmem, vmem),
            scratch_shapes=[pltpu.VMEM((3, rows + 8, TILE), f32), pltpu.VMEM((6, width, TILE), f32)],
            compiler_params=pltpu.CompilerParams(vmem_limit_bytes=32 << 20),
            cost_estimate=pl.CostEstimate(flops=5000 * work, bytes_accessed=16 * work, transcendentals=work),
            name="pairs",
        )(counts, lists, nod, ctl, csum)

    mine, csum = pairs(0, jnp.zeros((6, width), f32))
    got = []
    for step in range(1, len(CALLS)):
        got = [g[:, g.shape[1] // 2 :] for g in got], [g[:, : g.shape[1] // 2] for g in got]
        sent = swap(sum(got[0], mine), "ctl", SUM_BITS[step - 1])
        mine, csum = pairs(step, csum)
        csum, sent = lax.optimization_barrier((csum, sent))
        got = got[1] + [sent]
    keep = sum(got, mine)
    ckeep = csum
    node_bits = SUM_BITS[len(CALLS) - 1 :]
    for step, bit in enumerate(CTL_BITS[::-1]):
        span = ckeep.shape[1] // 2
        csend = swap(ckeep[:, span:], "vol", bit)
        if step < len(node_bits):
            size = keep.shape[1] // 2
            send = swap(keep[:, size:], "ctl", node_bits[step])
            csend, send = lax.optimization_barrier((csend, send))
            keep = keep[:, :size] + send
        ckeep = ckeep[:, :span] + csend
    node_grad = keep.reshape(3, 1, own) * (-20.0 / math.sqrt(total_ctl))
    weight_grad = ckeep[:3].reshape(3, 1, part) * (4.0 / math.sqrt(total_nodes))
    control_grad = ckeep[3:].reshape(3, 1, part) * (20.0 / math.sqrt(total_nodes))
    return (node_grad, weight_grad, control_grad)


def solution(mesh):
    nodes = P(None, "vol", "ctl")
    ctl = P(None, "ctl", "vol")
    return jax.shard_map(
        local,
        mesh=mesh,
        in_specs=(nodes, nodes, ctl, ctl, P("vol", None, "ctl", None)),
        out_specs=(nodes, ctl, ctl),
        check_vma=False,
    )
```

time: 101 us -> 91.4 us (0.905)
  waiting for transfers between devices: 22.6 us -> 15.9 us
  Pallas kernels: 44.1 us -> 38.3 us
  starting transfers between devices: 26.2 us -> 28.8 us
    ppermute x16, waiting for transfers between devices: 22.6 us -> 15.9 us  [swap(): lax.ppermute(value, axis, [(i, i ^ bit) for i in range(lax.axis_size(axis...]
    pallas_call x2 -> x3, Pallas kernels: 44.1 us -> 38.3 us  [the longest x2 36.1 us: pairs(): pl.pallas_call(functools.partial(pair_kernel, call=call, stride=stride, p...]
    ppermute x16, starting transfers between devices: 26.2 us -> 28.8 us  [swap(): lax.ppermute(value, axis, [(i, i ^ bit) for i in range(lax.axis_size(axis...]
    unnamed x17 -> x19, local copies, waits for them, and re-layouts: 3.12 us -> 1.99 us
  transfers between devices with their start and end apart: 16 -> 16, of which waited for: 9 -> 7; matrix products, arithmetic and copies ran while one was open for 4% -> 3% of each run, Pallas kernels for 6% -> 23%
where the time goes in v2:
time: 91.4 us; the launch traced here: 89.7 us
  Pallas kernels  38.3 us (42%)
  starting transfers between devices  28.8 us (32%)
  waiting for transfers between devices  15.9 us (17%)
  local copies, waits for them, and re-layouts  3.37 us (4%)
  other arithmetic  2.44 us (3%)
    pallas_call x2, Pallas kernels, pairs(): pl.pallas_call(functools.partial(pair_kernel, call=call, stride=stride, p...  36.1 us
    ppermute x16, starting transfers between devices, swap(): lax.ppermute(value, axis, [(i, i ^ bit) for i in range(lax.axis_size(axis...  28.8 us
    ppermute x16, waiting for transfers between devices, swap(): lax.ppermute(value, axis, [(i, i ^ bit) for i in range(lax.axis_size(axis...  15.9 us
    pallas_call x1, Pallas kernels, local(): pl.pallas_call(functools.partial(list_kernel, units=units, stride=stride)...  2.25 us
    unnamed x19, local copies, waits for them, and re-layouts  1.99 us
  transfers between devices with their start and end apart: 16, of which 7 were waited for; matrix products, arithmetic and copies ran while one was open for 3% of the time, Pallas kernels for 23%

profile of v2, /device:TPU:2, one launch (start us, length us, event | category | flops | bytes accessed | tf_op | source)
XLA Modules:
  0.0 89.7 jit_solution(9725920849463289445)
XLA Ops:
  0.6 0.8 pad_maximum_fusion.3
  1.4 0.0 copy-start.3
  1.4 0.0 copy-start.4
  1.5 1.6 %collective-permute-start = (f32[6,16,128]{2,1,0:T(8,128)S(1)}, f32[6,16,128]{2,1,0:T(8,128)S(1)}, u32[]{:S(2)}, u32[]{:S(2)}) collective-permute-start(f32[6,16,128]{2,1,0:T(8,128)S(1)} %bitcast.14), channel_id=1, source_target_pairs={{0,12},{1,13},{2,14},{3,15},{4,8},{5,9},{6,10},{7,11},{8,4},{9,5},... | collective-permute-start | bytes 147464 | tf_op jit(solution)/shard_map/ppermute | solution.py:34
  3.0 0.0 copy-done.3
  3.0 0.0 copy-done.4
  3.1 6.4 %collective-permute-start.4 = (f32[6,16]{1,0:T(8,128)S(1)}, f32[6,16]{1,0:T(8,128)S(1)}, u32[]{:S(2)}, u32[]{:S(2)}) collective-permute-start(f32[6,16]{1,0:T(8,128)S(1)} %maximum_bitcast_fusion), channel_id=1, source_target_pairs={{0,192},{16,208},{32,224},{48,240},{64,128},{80,144},{96,160},{112... | collective-permute-start | bytes 1160 | tf_op jit(solution)/shard_map/ppermute | solution.py:34
  9.5 0.0 copy-start.2
  9.5 0.7 pad_add_fusion.where_ref
  10.1 0.0 copy-done.2
  10.1 0.1 copy.13
  10.3 0.7 reshape.36.mask_ref
  11.0 0.0 collective-permute-done
  11.0 3.3 %collective-permute-start.1 = (f32[6,32,128]{2,1,0:T(8,128)S(1)}, f32[6,32,128]{2,1,0:T(8,128)S(1)}, u32[]{:S(2)}, u32[]{:S(2)}) collective-permute-start(f32[6,32,128]{2,1,0:T(8,128)S(1)} %pad_maximum_fusion.2), channel_id=1, source_target_pairs={{0,2},{1,3},{2,0},{3,1},{4,6},{5,7},{6,4},{7,5},{8,10},{9,11},{10,... | collective-permute-start | bytes 294920 | tf_op jit(solution)/shard_map/ppermute | solution.py:34
  14.3 0.0 collective-permute-done.4
  14.3 0.1 pad_maximum_fusion.4
  14.4 1.5 %collective-permute-start.5 = (f32[6,32]{1,0:T(8,128)S(1)}, f32[6,32]{1,0:T(8,128)S(1)}, u32[]{:S(2)}, u32[]{:S(2)}) collective-permute-start(f32[6,32]{1,0:T(8,128)S(1)} %pad_maximum_fusion.4), channel_id=1, source_target_pairs={{0,64},{16,80},{32,96},{48,112},{64,0},{80,16},{96,32},{112,48},{1... | collective-permute-start | bytes 2312 | tf_op jit(solution)/shard_map/ppermute | solution.py:34
  15.8 1.4 %collective-permute-done.1 = f32[6,32,128]{2,1,0:T(8,128)S(1)} collective-permute-done((f32[6,32,128]{2,1,0:T(8,128)S(1)}, f32[6,32,128]{2,1,0:T(8,128)S(1)}, u32[]{:S(2)}, u32[]{:S(2)}) %collective-permute-start.1) | collective-permute-done | bytes 98336 | tf_op jit(solution)/shard_map/ppermute | solution.py:34
  17.2 1.9 %collective-permute-start.2 = (f32[6,64,128]{2,1,0:T(8,128)S(1)}, f32[6,64,128]{2,1,0:T(8,128)S(1)}, u32[]{:S(2)}, u32[]{:S(2)}) collective-permute-start(f32[6,64,128]{2,1,0:T(8,128)S(1)} %pad_maximum_fusion.1), channel_id=1, source_target_pairs={{0,4},{1,5},{2,6},{3,7},{4,0},{5,1},{6,2},{7,3},{8,12},{9,13},{10,... | collective-permute-start | bytes 589832 | tf_op jit(solution)/shard_map/ppermute | solution.py:34
  19.1 0.0 collective-permute-done.5
  19.1 0.1 pad_maximum_fusion.5
  19.2 1.0 %collective-permute-start.6 = (f32[6,64]{1,0:T(8,128)S(1)}, f32[6,64]{1,0:T(8,128)S(1)}, u32[]{:S(2)}, u32[]{:S(2)}) collective-permute-start(f32[6,64]{1,0:T(8,128)S(1)} %pad_maximum_fusion.5), channel_id=1, source_target_pairs={{0,32},{16,48},{32,0},{48,16},{64,96},{80,112},{96,64},{112,80},{1... | collective-permute-start | bytes 4616 | tf_op jit(solution)/shard_map/ppermute | solution.py:34
  20.2 2.6 %collective-permute-done.6 = f32[6,64]{1,0:T(8,128)S(1)} collective-permute-done((f32[6,64]{1,0:T(8,128)S(1)}, f32[6,64]{1,0:T(8,128)S(1)}, u32[]{:S(2)}, u32[]{:S(2)}) %collective-permute-start.6) | collective-permute-done | bytes 1568 | tf_op jit(solution)/shard_map/ppermute | solution.py:34
  22.8 0.1 pad_maximum_fusion.6
  22.9 1.6 %collective-permute-start.7 = (f32[6,128]{1,0:T(8,128)S(1)}, f32[6,128]{1,0:T(8,128)S(1)}, u32[]{:S(2)}, u32[]{:S(2)}) collective-permute-start(f32[6,128]{1,0:T(8,128)S(1)} %pad_maximum_fusion.6), channel_id=1, source_target_pairs={{0,16},{16,0},{32,48},{48,32},{64,80},{80,64},{96,112},{112,96},{1... | collective-permute-start | bytes 9224 | tf_op jit(solution)/shard_map/ppermute | solution.py:34
  24.5 2.3 %kept_tiles.1 = (s32[544]{0:T(1024)}, s32[4]{0:T(128)}) custom-call(s32[2]{0:T(128)} %pad_add_fusion.where_ref, s32[512]{0:T(512)} %reshape.36.mask_ref), custom_call_target="tpu_custom_call" | custom-call | tf_op jit(solution)/shard_map/kept_tiles/pallas_call | solution.py:131
  26.8 0.0 collective-permute-done.2
  26.8 0.1 collective-permute-start.3
  26.9 0.0 collective-permute-done.7
  26.9 0.1 concatenate.45
  27.1 1.6 %collective-permute-done.3 = f32[6,128,128]{2,1,0:T(8,128)S(1)} collective-permute-done((f32[6,128,128]{2,1,0:T(8,128)S(1)}, f32[6,128,128]{2,1,0:T(8,128)S(1)}, u32[]{:S(2)}, u32[]{:S(2)}) %collective-permute-start.3) | collective-permute-done | bytes 393248 | tf_op jit(solution)/shard_map/ppermute | solution.py:34
  28.7 0.1 pad.4.nod_ref
  28.7 0.3 broadcast_in_dim.4.ctl_ref
  29.0 0.0 copy-start
  29.0 0.0 copy-start.1
  29.0 0.7 copy-done
  29.7 0.0 copy-done.1
  29.7 17.9 %pairs.2 = (f32[3,128,128]{2,1,0:T(8,128)S(1)}, f32[6,256]{1,0:T(8,128)S(1)}) custom-call(s32[4]{0:T(128)S(1)} %copy-done.1, s32[544]{0:T(1024)S(1)} %copy-done, f32[6,264,128]{2,1,0:T(8,128)S(1)} %pad.4.nod_ref, f32[6,256,128]{2,1,0:T(8,128)S(1)} %broadcast_in_dim.4.ctl_ref, f32[6,256]{1,0:T(8,128)S(1)} %broadcast_in_dim.10.before_ref), custom_call_target="tpu_custom_call" | custom-call | flops 20971520000 | bytes 67108864 | tf_op jit(solution)/shard_map/pairs/pallas_call | solution.py:150
  47.6 0.4 collective-permute-start.8
  48.0 18.2 %pairs.3 = (f32[3,128,128]{2,1,0:T(8,128)S(1)}, f32[6,256]{1,0:T(8,128)S(1)}) custom-call(s32[4]{0:T(128)S(1)} %copy-done.1, s32[544]{0:T(1024)S(1)} %copy-done, f32[6,264,128]{2,1,0:T(8,128)S(1)} %pad.4.nod_ref, f32[6,256,128]{2,1,0:T(8,128)S(1)} %broadcast_in_dim.4.ctl_ref, f32[6,256]{1,0:T(8,128)S(1)} %get-tuple-element.31.before_ref), custom_call_target="tpu_custom_call" | custom-call | flops 20971520000 | bytes 67108864 | tf_op jit(solution)/shard_map/pairs/pallas_call | solution.py:150
  66.2 0.0 collective-permute-done.8
  66.2 3.7 %collective-permute-start.10 = (f32[3,64,128]{2,1,0:T(8,128)S(1)}, f32[3,64,128]{2,1,0:T(8,128)S(1)}, u32[]{:S(2)}, u32[]{:S(2)}) collective-permute-start(f32[3,64,128]{2,1,0:T(8,128)S(1)} %slice.65), channel_id=1, source_target_pairs={{0,2},{1,3},{2,0},{3,1},{4,6},{5,7},{6,4},{7,5},{8,10},{9,11},{10,... | collective-permute-start | bytes 294920 | tf_op jit(solution)/shard_map/ppermute | solution.py:34
  69.9 0.1 collective-permute-start.9
  70.1 3.5 %collective-permute-done.9 = f32[6,128]{1,0:T(8,128)S(1)} collective-permute-done((f32[6,128]{1,0:T(8,128)S(1)}, f32[6,128]{1,0:T(8,128)S(1)}, u32[]{:S(2)}, u32[]{:S(2)}) %collective-permute-start.9) | collective-permute-done | bytes 3104 | tf_op jit(solution)/shard_map/ppermute | solution.py:34
  73.5 0.0 collective-permute-done.10
  73.6 0.7 collective-permute-start.12
  74.3 0.1 slice.53
  74.4 1.5 %collective-permute-start.11 = (f32[6,64]{1,0:T(8,128)S(1)}, f32[6,64]{1,0:T(8,128)S(1)}, u32[]{:S(2)}, u32[]{:S(2)}) collective-permute-start(f32[6,64]{1,0:T(8,128)S(1)} %slice.53), channel_id=1, source_target_pairs={{0,32},{16,48},{32,0},{48,16},{64,96},{80,112},{96,64},{112,80},{1... | collective-permute-start | bytes 4616 | tf_op jit(solution)/shard_map/ppermute | solution.py:34
  75.9 2.2 %collective-permute-done.11 = f32[6,64]{1,0:T(8,128)S(1)} collective-permute-done((f32[6,64]{1,0:T(8,128)S(1)}, f32[6,64]{1,0:T(8,128)S(1)}, u32[]{:S(2)}, u32[]{:S(2)}) %collective-permute-start.11) | collective-permute-done | bytes 1568 | tf_op jit(solution)/shard_map/ppermute | solution.py:34
  78.0 0.0 collective-permute-done.12
  78.1 0.1 collective-permute-start.14
  78.2 0.1 slice.57
  78.2 1.9 %collective-permute-start.13 = (f32[6,32]{1,0:T(8,128)S(1)}, f32[6,32]{1,0:T(8,128)S(1)}, u32[]{:S(2)}, u32[]{:S(2)}) collective-permute-start(f32[6,32]{1,0:T(8,128)S(1)} %slice.57), channel_id=1, source_target_pairs={{0,64},{16,80},{32,96},{48,112},{64,0},{80,16},{96,32},{112,48},{1... | collective-permute-start | bytes 2312 | tf_op jit(solution)/shard_map/ppermute | solution.py:34
  80.1 2.6 %collective-permute-done.13 = f32[6,32]{1,0:T(8,128)S(1)} collective-permute-done((f32[6,32]{1,0:T(8,128)S(1)}, f32[6,32]{1,0:T(8,128)S(1)}, u32[]{:S(2)}, u32[]{:S(2)}) %collective-permute-start.13) | collective-permute-done | bytes 800 | tf_op jit(solution)/shard_map/ppermute | solution.py:34
  82.8 0.0 collective-permute-done.14
  82.8 0.1 slice.61
  82.9 3.1 %collective-permute-start.15 = (f32[6,16]{1,0:T(8,128)S(1)}, f32[6,16]{1,0:T(8,128)S(1)}, u32[]{:S(2)}, u32[]{:S(2)}) collective-permute-start(f32[6,16]{1,0:T(8,128)S(1)} %slice.61), channel_id=1, source_target_pairs={{0,192},{16,208},{32,224},{48,240},{64,128},{80,144},{96,160},{112... | collective-permute-start | bytes 1160 | tf_op jit(solution)/shard_map/ppermute | solution.py:34
  85.9 0.6 fusion
  86.5 2.1 %collective-permute-done.15 = f32[6,16]{1,0:T(8,128)S(1)} collective-permute-done((f32[6,16]{1,0:T(8,128)S(1)}, f32[6,16]{1,0:T(8,128)S(1)}, u32[]{:S(2)}, u32[]{:S(2)}) %collective-permute-start.15) | collective-permute-done | bytes 416 | tf_op jit(solution)/shard_map/ppermute | solution.py:34
  88.6 0.6 copy.17
  89.2 0.6 copy.18
  (24 shorter events, 0.2 us)
Async XLA Ops:
  1.4 1.6 %copy-start.3 = (f32[3,1,16]{2,1,0:T(1,128)S(1)}, f32[3,1,16]{2,1,0:T(1,128)}, u32[]{:S(2)}) copy-start(f32[3,1,16]{2,1,0:T(1,128)} %param.7) | copy-start | bytes 580
  1.4 1.6 %copy-start.4 = (f32[3,1,16]{2,1,0:T(1,128)S(1)}, f32[3,1,16]{2,1,0:T(1,128)}, u32[]{:S(2)}) copy-start(f32[3,1,16]{2,1,0:T(1,128)} %param.8) | copy-start | bytes 580
  1.5 9.5 %collective-permute-start = (f32[6,16,128]{2,1,0:T(8,128)S(1)}, f32[6,16,128]{2,1,0:T(8,128)S(1)}, u32[]{:S(2)}, u32[]{:S(2)}) collective-permute-start(f32[6,16,128]{2,1,0:T(8,128)S(1)} %bitcast.14), channel_id=1, source_target_pairs={{0,12},{1,13},{2,14},{3,15},{4,8},{5,9},{6,10},{7,11},{8,4},{9,5},... | collective-permute-start | bytes 147464 | tf_op jit(solution)/shard_map/ppermute | solution.py:34
  3.1 11.2 %collective-permute-start.4 = (f32[6,16]{1,0:T(8,128)S(1)}, f32[6,16]{1,0:T(8,128)S(1)}, u32[]{:S(2)}, u32[]{:S(2)}) collective-permute-start(f32[6,16]{1,0:T(8,128)S(1)} %maximum_bitcast_fusion), channel_id=1, source_target_pairs={{0,192},{16,208},{32,224},{48,240},{64,128},{80,144},{96,160},{112... | collective-permute-start | bytes 1160 | tf_op jit(solution)/shard_map/ppermute | solution.py:34
  9.5 0.7 copy-start.2
  11.0 6.2 %collective-permute-start.1 = (f32[6,32,128]{2,1,0:T(8,128)S(1)}, f32[6,32,128]{2,1,0:T(8,128)S(1)}, u32[]{:S(2)}, u32[]{:S(2)}) collective-permute-start(f32[6,32,128]{2,1,0:T(8,128)S(1)} %pad_maximum_fusion.2), channel_id=1, source_target_pairs={{0,2},{1,3},{2,0},{3,1},{4,6},{5,7},{6,4},{7,5},{8,10},{9,11},{10,... | collective-permute-start | bytes 294920 | tf_op jit(solution)/shard_map/ppermute | solution.py:34
  14.4 4.8 %collective-permute-start.5 = (f32[6,32]{1,0:T(8,128)S(1)}, f32[6,32]{1,0:T(8,128)S(1)}, u32[]{:S(2)}, u32[]{:S(2)}) collective-permute-start(f32[6,32]{1,0:T(8,128)S(1)} %pad_maximum_fusion.4), channel_id=1, source_target_pairs={{0,64},{16,80},{32,96},{48,112},{64,0},{80,16},{96,32},{112,48},{1... | collective-permute-start | bytes 2312 | tf_op jit(solution)/shard_map/ppermute | solution.py:34
  17.2 9.5 %collective-permute-start.2 = (f32[6,64,128]{2,1,0:T(8,128)S(1)}, f32[6,64,128]{2,1,0:T(8,128)S(1)}, u32[]{:S(2)}, u32[]{:S(2)}) collective-permute-start(f32[6,64,128]{2,1,0:T(8,128)S(1)} %pad_maximum_fusion.1), channel_id=1, source_target_pairs={{0,4},{1,5},{2,6},{3,7},{4,0},{5,1},{6,2},{7,3},{8,12},{9,13},{10,... | collective-permute-start | bytes 589832 | tf_op jit(solution)/shard_map/ppermute | solution.py:34
  19.2 3.6 %collective-permute-start.6 = (f32[6,64]{1,0:T(8,128)S(1)}, f32[6,64]{1,0:T(8,128)S(1)}, u32[]{:S(2)}, u32[]{:S(2)}) collective-permute-start(f32[6,64]{1,0:T(8,128)S(1)} %pad_maximum_fusion.5), channel_id=1, source_target_pairs={{0,32},{16,48},{32,0},{48,16},{64,96},{80,112},{96,64},{112,80},{1... | collective-permute-start | bytes 4616 | tf_op jit(solution)/shard_map/ppermute | solution.py:34
  22.9 4.0 %collective-permute-start.7 = (f32[6,128]{1,0:T(8,128)S(1)}, f32[6,128]{1,0:T(8,128)S(1)}, u32[]{:S(2)}, u32[]{:S(2)}) collective-permute-start(f32[6,128]{1,0:T(8,128)S(1)} %pad_maximum_fusion.6), channel_id=1, source_target_pairs={{0,16},{16,0},{32,48},{48,32},{64,80},{80,64},{96,112},{112,96},{1... | collective-permute-start | bytes 9224 | tf_op jit(solution)/shard_map/ppermute | solution.py:34
  26.8 1.8 %collective-permute-start.3 = (f32[6,128,128]{2,1,0:T(8,128)S(1)}, f32[6,128,128]{2,1,0:T(8,128)S(1)}, u32[]{:S(2)}, u32[]{:S(2)}) collective-permute-start(f32[6,128,128]{2,1,0:T(8,128)S(1)} %pad_maximum_fusion), channel_id=1, source_target_pairs={{0,1},{1,0},{2,3},{3,2},{4,5},{5,4},{6,7},{7,6},{8,9},{9,8},{10,11... | collective-permute-start | bytes 1179656 | tf_op jit(solution)/shard_map/ppermute | solution.py:34
  29.0 0.7 copy-start
  29.0 0.7 copy-start.1
  47.6 18.6 %collective-permute-start.8 = (f32[3,128,128]{2,1,0:T(8,128)S(1)}, f32[3,128,128]{2,1,0:T(8,128)S(1)}, u32[]{:S(2)}, u32[]{:S(2)}) collective-permute-start(f32[3,128,128]{2,1,0:T(8,128)S(1)} %get-tuple-element.34), channel_id=1, source_target_pairs={{0,12},{1,13},{2,14},{3,15},{4,8},{5,9},{6,10},{7,11},{8,4},{9,5},... | collective-permute-start | bytes 589832 | tf_op jit(solution)/shard_map/ppermute | solution.py:34
  66.2 7.3 %collective-permute-start.10 = (f32[3,64,128]{2,1,0:T(8,128)S(1)}, f32[3,64,128]{2,1,0:T(8,128)S(1)}, u32[]{:S(2)}, u32[]{:S(2)}) collective-permute-start(f32[3,64,128]{2,1,0:T(8,128)S(1)} %slice.65), channel_id=1, source_target_pairs={{0,2},{1,3},{2,0},{3,1},{4,6},{5,7},{6,4},{7,5},{8,10},{9,11},{10,... | collective-permute-start | bytes 294920 | tf_op jit(solution)/shard_map/ppermute | solution.py:34
  69.9 3.6 %collective-permute-start.9 = (f32[6,128]{1,0:T(8,128)S(1)}, f32[6,128]{1,0:T(8,128)S(1)}, u32[]{:S(2)}, u32[]{:S(2)}) collective-permute-start(f32[6,128]{1,0:T(8,128)S(1)} %slice.49), channel_id=1, source_target_pairs={{0,16},{16,0},{32,48},{48,32},{64,80},{80,64},{96,112},{112,96},{1... | collective-permute-start | bytes 9224 | tf_op jit(solution)/shard_map/ppermute | solution.py:34
  73.6 4.5 %collective-permute-start.12 = (f32[3,32,128]{2,1,0:T(8,128)S(1)}, f32[3,32,128]{2,1,0:T(8,128)S(1)}, u32[]{:S(2)}, u32[]{:S(2)}) collective-permute-start(f32[3,32,128]{2,1,0:T(8,128)S(1)} %slice.67), channel_id=1, source_target_pairs={{0,4},{1,5},{2,6},{3,7},{4,0},{5,1},{6,2},{7,3},{8,12},{9,13},{10,... | collective-permute-start | bytes 147464 | tf_op jit(solution)/shard_map/ppermute | solution.py:34
  74.4 3.6 %collective-permute-start.11 = (f32[6,64]{1,0:T(8,128)S(1)}, f32[6,64]{1,0:T(8,128)S(1)}, u32[]{:S(2)}, u32[]{:S(2)}) collective-permute-start(f32[6,64]{1,0:T(8,128)S(1)} %slice.53), channel_id=1, source_target_pairs={{0,32},{16,48},{32,0},{48,16},{64,96},{80,112},{96,64},{112,80},{1... | collective-permute-start | bytes 4616 | tf_op jit(solution)/shard_map/ppermute | solution.py:34
  78.1 4.7 %collective-permute-start.14 = (f32[3,16,128]{2,1,0:T(8,128)S(1)}, f32[3,16,128]{2,1,0:T(8,128)S(1)}, u32[]{:S(2)}, u32[]{:S(2)}) collective-permute-start(f32[3,16,128]{2,1,0:T(8,128)S(1)} %slice.69), channel_id=1, source_target_pairs={{0,1},{1,0},{2,3},{3,2},{4,5},{5,4},{6,7},{7,6},{8,9},{9,8},{10,11... | collective-permute-start | bytes 73736 | tf_op jit(solution)/shard_map/ppermute | solution.py:34
  78.2 4.5 %collective-permute-start.13 = (f32[6,32]{1,0:T(8,128)S(1)}, f32[6,32]{1,0:T(8,128)S(1)}, u32[]{:S(2)}, u32[]{:S(2)}) collective-permute-start(f32[6,32]{1,0:T(8,128)S(1)} %slice.57), channel_id=1, source_target_pairs={{0,64},{16,80},{32,96},{48,112},{64,0},{80,16},{96,32},{112,48},{1... | collective-permute-start | bytes 2312 | tf_op jit(solution)/shard_map/ppermute | solution.py:34
  82.9 5.7 %collective-permute-start.15 = (f32[6,16]{1,0:T(8,128)S(1)}, f32[6,16]{1,0:T(8,128)S(1)}, u32[]{:S(2)}, u32[]{:S(2)}) collective-permute-start(f32[6,16]{1,0:T(8,128)S(1)} %slice.61), channel_id=1, source_target_pairs={{0,192},{16,208},{32,224},{48,240},{64,128},{80,144},{96,160},{112... | collective-permute-start | bytes 1160 | tf_op jit(solution)/shard_map/ppermute | solution.py:34

commit v3 on v2

--- a/solution.py
+++ b/solution.py
@@ -49,10 +49,8 @@
                 call, half = lists[j]
                 list_ref[found[j]] = (place(CALLS[call][0] + i) * units + k) * SHIFT + i * units + k
                 found[j] = found[j] + mask_ref[rows[j] + 2 * k]
-    for j, (call, half) in enumerate(lists):
-        for k in range(GROUP):
-            list_ref[found[j] + k] = (units << len(NODE_BITS)) * SHIFT + CALLS[call][1] * units
-        count_ref[j] = (found[j] - j * stride + GROUP - 1) // GROUP
+    for j in range(len(lists)):
+        count_ref[j] = found[j] - j * stride
 
 
 def pair_kernel(count_ref, list_ref, nod_ref, ctl_ref, before_ref, part_ref, csum_ref, node_ref, acc_ref, *, call, stride, part):
@@ -62,17 +60,17 @@
         row = 2 * call + half
         starts = [s for s in range(0, acc_ref.shape[1], 8) if s // part % 2 == half]
 
-        def body(i, _, row=row, starts=starts):
-            items = [list_ref[row * stride + i * GROUP + b] for b in range(GROUP)]
+        def body(first, size, row=row, starts=starts):
+            items = [list_ref[row * stride + first + b] for b in range(size)]
             ts = [item >> 10 for item in items]
             outs = [item & (SHIFT - 1) for item in items]
             xg = [[jnp.broadcast_to(nod_ref[k, pl.ds(t, 1), :], (8, TILE)) for k in range(6)] for t in ts]
-            node_sum = [[None] * 3 for _ in range(GROUP)]
+            node_sum = [[None] * 3 for _ in range(size)]
             for c, start in enumerate(starts):
                 rows = pl.ds(start, 8)
                 yw = [ctl_ref[k, rows, :] for k in range(6)]
                 ctl_sum = [None] * 6
-                for b in range(GROUP):
+                for b in range(size):
                     x = xg[b][:3]
                     g = xg[b][3:]
                     diff = [x[k] - yw[k] for k in range(3)]
@@ -91,12 +89,21 @@
                         ctl_sum[k] = pushed if b == 0 else ctl_sum[k] + pushed
                 for k in range(6):
                     acc_ref[k, rows, :] += ctl_sum[k]
-            for b in range(GROUP):
+            for b in range(size):
                 for k in range(3):
                     node_ref[k, pl.ds(outs[b], 1), :] += jnp.sum(node_sum[b][k], axis=0, keepdims=True)
+
+        def group(i, _, body=body):
+            body(i * GROUP, GROUP)
             return 0
 
-        lax.fori_loop(0, count_ref[row], body, 0)
+        def single(i, _, body=body):
+            body(i, 1)
+            return 0
+
+        count = count_ref[row]
+        lax.fori_loop(0, count // GROUP, group, 0)
+        lax.fori_loop(count // GROUP * GROUP, count, single, 0)
     part_ref[...] = node_ref[:, : part_ref.shape[1], :]
     for k in range(6):
         for s in range(0, acc_ref.shape[1], TILE):
@@ -168,17 +175,24 @@
         got = got[1] + [sent]
     keep = sum(got, mine)
     ckeep = csum
-    node_bits = SUM_BITS[len(CALLS) - 1 :]
+    sent = []
     for step, bit in enumerate(CTL_BITS[::-1]):
         span = ckeep.shape[1] // 2
         csend = swap(ckeep[:, span:], "vol", bit)
-        if step < len(node_bits):
+        if sent:
+            if step < len(CTL_BITS) - 1:
+                csend, *sent = lax.optimization_barrier((csend, *sent))
+            keep = sent[0] + sent[1]
+        sent = []
+        if len(CALLS) - 1 + step < len(SUM_BITS):
             size = keep.shape[1] // 2
-            send = swap(keep[:, size:], "ctl", node_bits[step])
-            csend, send = lax.optimization_barrier((csend, send))
-            keep = keep[:, :size] + send
-        ckeep = ckeep[:, :span] + csend
+            sent = [keep[:, :size], swap(keep[:, size:], "ctl", SUM_BITS[len(CALLS) - 1 + step])]
+        if step < len(CTL_BITS) - 1:
+            ckeep = ckeep[:, :span] + csend
+    if sent:
+        keep = sent[0] + sent[1]
     node_grad = keep.reshape(3, 1, own) * (-20.0 / math.sqrt(total_ctl))
+    ckeep = ckeep[:, :span] + csend
     weight_grad = ckeep[:3].reshape(3, 1, part) * (4.0 / math.sqrt(total_nodes))
     control_grad = ckeep[3:].reshape(3, 1, part) * (20.0 / math.sqrt(total_nodes))
     return (node_grad, weight_grad, control_grad)

time: 91.4 us -> 89 us (0.974)
  Pallas kernels: 38.3 us -> 36.8 us
  waiting for transfers between devices: 15.9 us -> 14.8 us
    pallas_call x2, Pallas kernels: 36.1 us -> 34.6 us  [pairs(): pl.pallas_call(functools.partial(pair_kernel, call=call, stride=stride, p...]
    ppermute x16, waiting for transfers between devices: 15.9 us -> 14.8 us  [swap(): lax.ppermute(value, axis, [(i, i ^ bit) for i in range(lax.axis_size(axis...]
  transfers between devices with their start and end apart: 16 -> 16, of which waited for: 7 -> 6; matrix products, arithmetic and copies ran while one was open for 3% -> 4% of each run, Pallas kernels for 23% -> 22%
where the time goes in v3:
time: 89 us; the launch traced here: 88 us
  Pallas kernels  36.8 us (41%)
  starting transfers between devices  29.7 us (33%)
  waiting for transfers between devices  14.8 us (17%)
  local copies, waits for them, and re-layouts  3.42 us (4%)
  other arithmetic  2.42 us (3%)
    pallas_call x2, Pallas kernels, pairs(): pl.pallas_call(functools.partial(pair_kernel, call=call, stride=stride, p...  34.6 us
    ppermute x16, starting transfers between devices, swap(): lax.ppermute(value, axis, [(i, i ^ bit) for i in range(lax.axis_size(axis...  29.7 us
    ppermute x16, waiting for transfers between devices, swap(): lax.ppermute(value, axis, [(i, i ^ bit) for i in range(lax.axis_size(axis...  14.8 us
    pallas_call x1, Pallas kernels, local(): pl.pallas_call(functools.partial(list_kernel, units=units, stride=stride)...  2.24 us
    unnamed x19, local copies, waits for them, and re-layouts  2.01 us
  transfers between devices with their start and end apart: 16, of which 6 were waited for; matrix products, arithmetic and copies ran while one was open for 4% of the time, Pallas kernels for 22%

profile of v3, /device:TPU:2, one launch (start us, length us, event | category | flops | bytes accessed | tf_op | source)
XLA Modules:
  0.0 88.0 jit_solution(10952300086530028576)
XLA Ops:
  0.6 0.8 pad_maximum_fusion.3
  1.4 0.0 copy-start.3
  1.4 0.0 copy-start.4
  1.5 1.6 %collective-permute-start = (f32[6,16,128]{2,1,0:T(8,128)S(1)}, f32[6,16,128]{2,1,0:T(8,128)S(1)}, u32[]{:S(2)}, u32[]{:S(2)}) collective-permute-start(f32[6,16,128]{2,1,0:T(8,128)S(1)} %bitcast.14), channel_id=1, source_target_pairs={{0,12},{1,13},{2,14},{3,15},{4,8},{5,9},{6,10},{7,11},{8,4},{9,5},... | collective-permute-start | bytes 147464 | tf_op jit(solution)/shard_map/ppermute | solution.py:34
  3.0 0.0 copy-done.3
  3.0 0.0 copy-done.4
  3.1 6.4 %collective-permute-start.4 = (f32[6,16]{1,0:T(8,128)S(1)}, f32[6,16]{1,0:T(8,128)S(1)}, u32[]{:S(2)}, u32[]{:S(2)}) collective-permute-start(f32[6,16]{1,0:T(8,128)S(1)} %maximum_bitcast_fusion), channel_id=1, source_target_pairs={{0,192},{16,208},{32,224},{48,240},{64,128},{80,144},{96,160},{112... | collective-permute-start | bytes 1160 | tf_op jit(solution)/shard_map/ppermute | solution.py:34
  9.5 0.0 copy-start.2
  9.5 0.6 pad_add_fusion.where_ref
  10.1 0.0 copy-done.2
  10.1 0.1 copy.13
  10.3 0.7 reshape.36.mask_ref
  11.0 0.0 collective-permute-done
  11.0 3.3 %collective-permute-start.1 = (f32[6,32,128]{2,1,0:T(8,128)S(1)}, f32[6,32,128]{2,1,0:T(8,128)S(1)}, u32[]{:S(2)}, u32[]{:S(2)}) collective-permute-start(f32[6,32,128]{2,1,0:T(8,128)S(1)} %pad_maximum_fusion.2), channel_id=1, source_target_pairs={{0,2},{1,3},{2,0},{3,1},{4,6},{5,7},{6,4},{7,5},{8,10},{9,11},{10,... | collective-permute-start | bytes 294920 | tf_op jit(solution)/shard_map/ppermute | solution.py:34
  14.3 0.0 collective-permute-done.4
  14.3 0.1 pad_maximum_fusion.4
  14.4 1.5 %collective-permute-start.5 = (f32[6,32]{1,0:T(8,128)S(1)}, f32[6,32]{1,0:T(8,128)S(1)}, u32[]{:S(2)}, u32[]{:S(2)}) collective-permute-start(f32[6,32]{1,0:T(8,128)S(1)} %pad_maximum_fusion.4), channel_id=1, source_target_pairs={{0,64},{16,80},{32,96},{48,112},{64,0},{80,16},{96,32},{112,48},{1... | collective-permute-start | bytes 2312 | tf_op jit(solution)/shard_map/ppermute | solution.py:34
  15.9 1.4 %collective-permute-done.1 = f32[6,32,128]{2,1,0:T(8,128)S(1)} collective-permute-done((f32[6,32,128]{2,1,0:T(8,128)S(1)}, f32[6,32,128]{2,1,0:T(8,128)S(1)}, u32[]{:S(2)}, u32[]{:S(2)}) %collective-permute-start.1) | collective-permute-done | bytes 98336 | tf_op jit(solution)/shard_map/ppermute | solution.py:34
  17.2 1.9 %collective-permute-start.2 = (f32[6,64,128]{2,1,0:T(8,128)S(1)}, f32[6,64,128]{2,1,0:T(8,128)S(1)}, u32[]{:S(2)}, u32[]{:S(2)}) collective-permute-start(f32[6,64,128]{2,1,0:T(8,128)S(1)} %pad_maximum_fusion.1), channel_id=1, source_target_pairs={{0,4},{1,5},{2,6},{3,7},{4,0},{5,1},{6,2},{7,3},{8,12},{9,13},{10,... | collective-permute-start | bytes 589832 | tf_op jit(solution)/shard_map/ppermute | solution.py:34
  19.1 0.0 collective-permute-done.5
  19.1 0.1 pad_maximum_fusion.5
  19.2 1.0 %collective-permute-start.6 = (f32[6,64]{1,0:T(8,128)S(1)}, f32[6,64]{1,0:T(8,128)S(1)}, u32[]{:S(2)}, u32[]{:S(2)}) collective-permute-start(f32[6,64]{1,0:T(8,128)S(1)} %pad_maximum_fusion.5), channel_id=1, source_target_pairs={{0,32},{16,48},{32,0},{48,16},{64,96},{80,112},{96,64},{112,80},{1... | collective-permute-start | bytes 4616 | tf_op jit(solution)/shard_map/ppermute | solution.py:34
  20.3 2.6 %collective-permute-done.6 = f32[6,64]{1,0:T(8,128)S(1)} collective-permute-done((f32[6,64]{1,0:T(8,128)S(1)}, f32[6,64]{1,0:T(8,128)S(1)}, u32[]{:S(2)}, u32[]{:S(2)}) %collective-permute-start.6) | collective-permute-done | bytes 1568 | tf_op jit(solution)/shard_map/ppermute | solution.py:34
  22.8 0.1 pad_maximum_fusion.6
  22.9 1.6 %collective-permute-start.7 = (f32[6,128]{1,0:T(8,128)S(1)}, f32[6,128]{1,0:T(8,128)S(1)}, u32[]{:S(2)}, u32[]{:S(2)}) collective-permute-start(f32[6,128]{1,0:T(8,128)S(1)} %pad_maximum_fusion.6), channel_id=1, source_target_pairs={{0,16},{16,0},{32,48},{48,32},{64,80},{80,64},{96,112},{112,96},{1... | collective-permute-start | bytes 9224 | tf_op jit(solution)/shard_map/ppermute | solution.py:34
  24.5 2.2 %kept_tiles.1 = (s32[544]{0:T(1024)}, s32[4]{0:T(128)}) custom-call(s32[2]{0:T(128)} %pad_add_fusion.where_ref, s32[512]{0:T(512)} %reshape.36.mask_ref), custom_call_target="tpu_custom_call" | custom-call | tf_op jit(solution)/shard_map/kept_tiles/pallas_call | solution.py:138
  26.8 0.0 collective-permute-done.2
  26.8 0.1 collective-permute-start.3
  26.9 0.0 collective-permute-done.7
  26.9 0.1 concatenate.45
  27.1 1.6 %collective-permute-done.3 = f32[6,128,128]{2,1,0:T(8,128)S(1)} collective-permute-done((f32[6,128,128]{2,1,0:T(8,128)S(1)}, f32[6,128,128]{2,1,0:T(8,128)S(1)}, u32[]{:S(2)}, u32[]{:S(2)}) %collective-permute-start.3) | collective-permute-done | bytes 393248 | tf_op jit(solution)/shard_map/ppermute | solution.py:34
  28.7 0.1 pad.4.nod_ref
  28.7 0.3 broadcast_in_dim.4.ctl_ref
  29.0 0.0 copy-start
  29.0 0.0 copy-start.1
  29.0 0.7 copy-done
  29.7 0.0 copy-done.1
  29.7 17.5 %pairs.2 = (f32[3,128,128]{2,1,0:T(8,128)S(1)}, f32[6,256]{1,0:T(8,128)S(1)}) custom-call(s32[4]{0:T(128)S(1)} %copy-done.1, s32[544]{0:T(1024)S(1)} %copy-done, f32[6,264,128]{2,1,0:T(8,128)S(1)} %pad.4.nod_ref, f32[6,256,128]{2,1,0:T(8,128)S(1)} %broadcast_in_dim.4.ctl_ref, f32[6,256]{1,0:T(8,128)S(1)} %broadcast_in_dim.10.before_ref), custom_call_target="tpu_custom_call" | custom-call | flops 20971520000 | bytes 67108864 | tf_op jit(solution)/shard_map/pairs/pallas_call | solution.py:157
  47.2 0.4 collective-permute-start.8
  47.6 17.1 %pairs.3 = (f32[3,128,128]{2,1,0:T(8,128)S(1)}, f32[6,256]{1,0:T(8,128)S(1)}) custom-call(s32[4]{0:T(128)S(1)} %copy-done.1, s32[544]{0:T(1024)S(1)} %copy-done, f32[6,264,128]{2,1,0:T(8,128)S(1)} %pad.4.nod_ref, f32[6,256,128]{2,1,0:T(8,128)S(1)} %broadcast_in_dim.4.ctl_ref, f32[6,256]{1,0:T(8,128)S(1)} %get-tuple-element.31.before_ref), custom_call_target="tpu_custom_call" | custom-call | flops 20971520000 | bytes 67108864 | tf_op jit(solution)/shard_map/pairs/pallas_call | solution.py:157
  64.7 0.0 collective-permute-done.8
  64.7 2.8 %collective-permute-start.9 = (f32[6,128]{1,0:T(8,128)S(1)}, f32[6,128]{1,0:T(8,128)S(1)}, u32[]{:S(2)}, u32[]{:S(2)}) collective-permute-start(f32[6,128]{1,0:T(8,128)S(1)} %slice.49), channel_id=1, source_target_pairs={{0,16},{16,0},{32,48},{48,32},{64,80},{80,64},{96,112},{112,96},{1... | collective-permute-start | bytes 9224 | tf_op jit(solution)/shard_map/ppermute | solution.py:34
  67.6 2.7 %collective-permute-start.11 = (f32[3,64,128]{2,1,0:T(8,128)S(1)}, f32[3,64,128]{2,1,0:T(8,128)S(1)}, u32[]{:S(2)}, u32[]{:S(2)}) collective-permute-start(f32[3,64,128]{2,1,0:T(8,128)S(1)} %get-tuple-element.49), channel_id=1, source_target_pairs={{0,2},{1,3},{2,0},{3,1},{4,6},{5,7},{6,4},{7,5},{8,10},{9,11},{10,... | collective-permute-start | bytes 294920 | tf_op jit(solution)/shard_map/ppermute | solution.py:34
  70.3 0.0 collective-permute-done.9
  70.3 0.1 slice.51
  70.4 0.9 %collective-permute-start.10 = (f32[6,64]{1,0:T(8,128)S(1)}, f32[6,64]{1,0:T(8,128)S(1)}, u32[]{:S(2)}, u32[]{:S(2)}) collective-permute-start(f32[6,64]{1,0:T(8,128)S(1)} %slice.51), channel_id=1, source_target_pairs={{0,32},{16,48},{32,0},{48,16},{64,96},{80,112},{96,64},{112,80},{1... | collective-permute-start | bytes 4616 | tf_op jit(solution)/shard_map/ppermute | solution.py:34
  71.3 2.7 %collective-permute-done.10 = f32[6,64]{1,0:T(8,128)S(1)} collective-permute-done((f32[6,64]{1,0:T(8,128)S(1)}, f32[6,64]{1,0:T(8,128)S(1)}, u32[]{:S(2)}, u32[]{:S(2)}) %collective-permute-start.10) | collective-permute-done | bytes 1568 | tf_op jit(solution)/shard_map/ppermute | solution.py:34
  74.0 0.0 collective-permute-done.11
  74.1 1.7 %collective-permute-start.13 = (f32[3,32,128]{2,1,0:T(8,128)S(1)}, f32[3,32,128]{2,1,0:T(8,128)S(1)}, u32[]{:S(2)}, u32[]{:S(2)}) collective-permute-start(f32[3,32,128]{2,1,0:T(8,128)S(1)} %get-tuple-element.51), channel_id=1, source_target_pairs={{0,4},{1,5},{2,6},{3,7},{4,0},{5,1},{6,2},{7,3},{8,12},{9,13},{10,... | collective-permute-start | bytes 147464 | tf_op jit(solution)/shard_map/ppermute | solution.py:34
  75.8 0.1 slice.54
  75.9 1.1 %collective-permute-start.12 = (f32[6,32]{1,0:T(8,128)S(1)}, f32[6,32]{1,0:T(8,128)S(1)}, u32[]{:S(2)}, u32[]{:S(2)}) collective-permute-start(f32[6,32]{1,0:T(8,128)S(1)} %slice.54), channel_id=1, source_target_pairs={{0,64},{16,80},{32,96},{48,112},{64,0},{80,16},{96,32},{112,48},{1... | collective-permute-start | bytes 2312 | tf_op jit(solution)/shard_map/ppermute | solution.py:34
  77.0 3.4 %collective-permute-done.12 = f32[6,32]{1,0:T(8,128)S(1)} collective-permute-done((f32[6,32]{1,0:T(8,128)S(1)}, f32[6,32]{1,0:T(8,128)S(1)}, u32[]{:S(2)}, u32[]{:S(2)}) %collective-permute-start.12) | collective-permute-done | bytes 800 | tf_op jit(solution)/shard_map/ppermute | solution.py:34
  80.4 0.0 collective-permute-done.13
  80.4 0.1 slice.61
  80.5 2.5 %collective-permute-start.15 = (f32[6,16]{1,0:T(8,128)S(1)}, f32[6,16]{1,0:T(8,128)S(1)}, u32[]{:S(2)}, u32[]{:S(2)}) collective-permute-start(f32[6,16]{1,0:T(8,128)S(1)} %slice.61), channel_id=1, source_target_pairs={{0,192},{16,208},{32,224},{48,240},{64,128},{80,144},{96,160},{112... | collective-permute-start | bytes 1160 | tf_op jit(solution)/shard_map/ppermute | solution.py:34
  83.0 0.1 collective-permute-start.14
  83.1 3.1 %collective-permute-done.15 = f32[6,16]{1,0:T(8,128)S(1)} collective-permute-done((f32[6,16]{1,0:T(8,128)S(1)}, f32[6,16]{1,0:T(8,128)S(1)}, u32[]{:S(2)}, u32[]{:S(2)}) %collective-permute-start.15) | collective-permute-done | bytes 416 | tf_op jit(solution)/shard_map/ppermute | solution.py:34
  86.2 0.6 copy.17
  86.8 0.6 copy.18
  87.4 0.0 collective-permute-done.14
  87.4 0.6 fusion
  (24 shorter events, 0.2 us)
Async XLA Ops:
  1.4 1.6 %copy-start.3 = (f32[3,1,16]{2,1,0:T(1,128)S(1)}, f32[3,1,16]{2,1,0:T(1,128)}, u32[]{:S(2)}) copy-start(f32[3,1,16]{2,1,0:T(1,128)} %param.7) | copy-start | bytes 580
  1.4 1.6 %copy-start.4 = (f32[3,1,16]{2,1,0:T(1,128)S(1)}, f32[3,1,16]{2,1,0:T(1,128)}, u32[]{:S(2)}) copy-start(f32[3,1,16]{2,1,0:T(1,128)} %param.8) | copy-start | bytes 580
  1.5 9.5 %collective-permute-start = (f32[6,16,128]{2,1,0:T(8,128)S(1)}, f32[6,16,128]{2,1,0:T(8,128)S(1)}, u32[]{:S(2)}, u32[]{:S(2)}) collective-permute-start(f32[6,16,128]{2,1,0:T(8,128)S(1)} %bitcast.14), channel_id=1, source_target_pairs={{0,12},{1,13},{2,14},{3,15},{4,8},{5,9},{6,10},{7,11},{8,4},{9,5},... | collective-permute-start | bytes 147464 | tf_op jit(solution)/shard_map/ppermute | solution.py:34
  3.1 11.2 %collective-permute-start.4 = (f32[6,16]{1,0:T(8,128)S(1)}, f32[6,16]{1,0:T(8,128)S(1)}, u32[]{:S(2)}, u32[]{:S(2)}) collective-permute-start(f32[6,16]{1,0:T(8,128)S(1)} %maximum_bitcast_fusion), channel_id=1, source_target_pairs={{0,192},{16,208},{32,224},{48,240},{64,128},{80,144},{96,160},{112... | collective-permute-start | bytes 1160 | tf_op jit(solution)/shard_map/ppermute | solution.py:34
  9.5 0.7 copy-start.2
  11.0 6.2 %collective-permute-start.1 = (f32[6,32,128]{2,1,0:T(8,128)S(1)}, f32[6,32,128]{2,1,0:T(8,128)S(1)}, u32[]{:S(2)}, u32[]{:S(2)}) collective-permute-start(f32[6,32,128]{2,1,0:T(8,128)S(1)} %pad_maximum_fusion.2), channel_id=1, source_target_pairs={{0,2},{1,3},{2,0},{3,1},{4,6},{5,7},{6,4},{7,5},{8,10},{9,11},{10,... | collective-permute-start | bytes 294920 | tf_op jit(solution)/shard_map/ppermute | solution.py:34
  14.4 4.8 %collective-permute-start.5 = (f32[6,32]{1,0:T(8,128)S(1)}, f32[6,32]{1,0:T(8,128)S(1)}, u32[]{:S(2)}, u32[]{:S(2)}) collective-permute-start(f32[6,32]{1,0:T(8,128)S(1)} %pad_maximum_fusion.4), channel_id=1, source_target_pairs={{0,64},{16,80},{32,96},{48,112},{64,0},{80,16},{96,32},{112,48},{1... | collective-permute-start | bytes 2312 | tf_op jit(solution)/shard_map/ppermute | solution.py:34
  17.2 9.5 %collective-permute-start.2 = (f32[6,64,128]{2,1,0:T(8,128)S(1)}, f32[6,64,128]{2,1,0:T(8,128)S(1)}, u32[]{:S(2)}, u32[]{:S(2)}) collective-permute-start(f32[6,64,128]{2,1,0:T(8,128)S(1)} %pad_maximum_fusion.1), channel_id=1, source_target_pairs={{0,4},{1,5},{2,6},{3,7},{4,0},{5,1},{6,2},{7,3},{8,12},{9,13},{10,... | collective-permute-start | bytes 589832 | tf_op jit(solution)/shard_map/ppermute | solution.py:34
  19.2 3.6 %collective-permute-start.6 = (f32[6,64]{1,0:T(8,128)S(1)}, f32[6,64]{1,0:T(8,128)S(1)}, u32[]{:S(2)}, u32[]{:S(2)}) collective-permute-start(f32[6,64]{1,0:T(8,128)S(1)} %pad_maximum_fusion.5), channel_id=1, source_target_pairs={{0,32},{16,48},{32,0},{48,16},{64,96},{80,112},{96,64},{112,80},{1... | collective-permute-start | bytes 4616 | tf_op jit(solution)/shard_map/ppermute | solution.py:34
  22.9 4.0 %collective-permute-start.7 = (f32[6,128]{1,0:T(8,128)S(1)}, f32[6,128]{1,0:T(8,128)S(1)}, u32[]{:S(2)}, u32[]{:S(2)}) collective-permute-start(f32[6,128]{1,0:T(8,128)S(1)} %pad_maximum_fusion.6), channel_id=1, source_target_pairs={{0,16},{16,0},{32,48},{48,32},{64,80},{80,64},{96,112},{112,96},{1... | collective-permute-start | bytes 9224 | tf_op jit(solution)/shard_map/ppermute | solution.py:34
  26.8 1.8 %collective-permute-start.3 = (f32[6,128,128]{2,1,0:T(8,128)S(1)}, f32[6,128,128]{2,1,0:T(8,128)S(1)}, u32[]{:S(2)}, u32[]{:S(2)}) collective-permute-start(f32[6,128,128]{2,1,0:T(8,128)S(1)} %pad_maximum_fusion), channel_id=1, source_target_pairs={{0,1},{1,0},{2,3},{3,2},{4,5},{5,4},{6,7},{7,6},{8,9},{9,8},{10,11... | collective-permute-start | bytes 1179656 | tf_op jit(solution)/shard_map/ppermute | solution.py:34
  29.0 0.7 copy-start
  29.0 0.7 copy-start.1
  47.2 17.5 %collective-permute-start.8 = (f32[3,128,128]{2,1,0:T(8,128)S(1)}, f32[3,128,128]{2,1,0:T(8,128)S(1)}, u32[]{:S(2)}, u32[]{:S(2)}) collective-permute-start(f32[3,128,128]{2,1,0:T(8,128)S(1)} %get-tuple-element.33), channel_id=1, source_target_pairs={{0,12},{1,13},{2,14},{3,15},{4,8},{5,9},{6,10},{7,11},{8,4},{9,5},... | collective-permute-start | bytes 589832 | tf_op jit(solution)/shard_map/ppermute | solution.py:34
  64.7 5.6 %collective-permute-start.9 = (f32[6,128]{1,0:T(8,128)S(1)}, f32[6,128]{1,0:T(8,128)S(1)}, u32[]{:S(2)}, u32[]{:S(2)}) collective-permute-start(f32[6,128]{1,0:T(8,128)S(1)} %slice.49), channel_id=1, source_target_pairs={{0,16},{16,0},{32,48},{48,32},{64,80},{80,64},{96,112},{112,96},{1... | collective-permute-start | bytes 9224 | tf_op jit(solution)/shard_map/ppermute | solution.py:34
  67.6 6.5 %collective-permute-start.11 = (f32[3,64,128]{2,1,0:T(8,128)S(1)}, f32[3,64,128]{2,1,0:T(8,128)S(1)}, u32[]{:S(2)}, u32[]{:S(2)}) collective-permute-start(f32[3,64,128]{2,1,0:T(8,128)S(1)} %get-tuple-element.49), channel_id=1, source_target_pairs={{0,2},{1,3},{2,0},{3,1},{4,6},{5,7},{6,4},{7,5},{8,10},{9,11},{10,... | collective-permute-start | bytes 294920 | tf_op jit(solution)/shard_map/ppermute | solution.py:34
  70.4 3.6 %collective-permute-start.10 = (f32[6,64]{1,0:T(8,128)S(1)}, f32[6,64]{1,0:T(8,128)S(1)}, u32[]{:S(2)}, u32[]{:S(2)}) collective-permute-start(f32[6,64]{1,0:T(8,128)S(1)} %slice.51), channel_id=1, source_target_pairs={{0,32},{16,48},{32,0},{48,16},{64,96},{80,112},{96,64},{112,80},{1... | collective-permute-start | bytes 4616 | tf_op jit(solution)/shard_map/ppermute | solution.py:34
  74.1 6.3 %collective-permute-start.13 = (f32[3,32,128]{2,1,0:T(8,128)S(1)}, f32[3,32,128]{2,1,0:T(8,128)S(1)}, u32[]{:S(2)}, u32[]{:S(2)}) collective-permute-start(f32[3,32,128]{2,1,0:T(8,128)S(1)} %get-tuple-element.51), channel_id=1, source_target_pairs={{0,4},{1,5},{2,6},{3,7},{4,0},{5,1},{6,2},{7,3},{8,12},{9,13},{10,... | collective-permute-start | bytes 147464 | tf_op jit(solution)/shard_map/ppermute | solution.py:34
  75.9 4.5 %collective-permute-start.12 = (f32[6,32]{1,0:T(8,128)S(1)}, f32[6,32]{1,0:T(8,128)S(1)}, u32[]{:S(2)}, u32[]{:S(2)}) collective-permute-start(f32[6,32]{1,0:T(8,128)S(1)} %slice.54), channel_id=1, source_target_pairs={{0,64},{16,80},{32,96},{48,112},{64,0},{80,16},{96,32},{112,48},{1... | collective-permute-start | bytes 2312 | tf_op jit(solution)/shard_map/ppermute | solution.py:34
  80.5 5.7 %collective-permute-start.15 = (f32[6,16]{1,0:T(8,128)S(1)}, f32[6,16]{1,0:T(8,128)S(1)}, u32[]{:S(2)}, u32[]{:S(2)}) collective-permute-start(f32[6,16]{1,0:T(8,128)S(1)} %slice.61), channel_id=1, source_target_pairs={{0,192},{16,208},{32,224},{48,240},{64,128},{80,144},{96,160},{112... | collective-permute-start | bytes 1160 | tf_op jit(solution)/shard_map/ppermute | solution.py:34
  83.0 4.3 %collective-permute-start.14 = (f32[3,16,128]{2,1,0:T(8,128)S(1)}, f32[3,16,128]{2,1,0:T(8,128)S(1)}, u32[]{:S(2)}, u32[]{:S(2)}) collective-permute-start(f32[3,16,128]{2,1,0:T(8,128)S(1)} %slice.69), channel_id=1, source_target_pairs={{0,1},{1,0},{2,3},{3,2},{4,5},{5,4},{6,7},{7,6},{8,9},{9,8},{10,11... | collective-permute-start | bytes 73736 | tf_op jit(solution)/shard_map/ppermute | solution.py:34

commit v4 on v3

--- a/solution.py
+++ b/solution.py
@@ -34,26 +34,27 @@
     return lax.ppermute(value, axis, [(i, i ^ bit) for i in range(lax.axis_size(axis))])
 
 
-def list_kernel(where_ref, mask_ref, list_ref, count_ref, *, units, stride):
+def list_kernel(mask_ref, list_ref, *, units, stride, tall):
     lists = [(call, half) for call in range(len(CALLS)) for half in range(2)]
     found = [jnp.int32(j * stride) for j in range(len(lists))]
-    columns = [half ^ where_ref[1] for half in range(2)]
+    mine = lax.axis_index("ctl")
+    columns = [half ^ (lax.axis_index("vol") // tall) for half in range(2)]
     for i in range(max(blocks for _, blocks in CALLS)):
         live = [j for j, (call, _) in enumerate(lists) if i < CALLS[call][1]]
         rows = {}
         for j in live:
             call, half = lists[j]
-            rows[j] = (where_ref[0] ^ offset(CALLS[call][0] + i)) * (2 * units) + columns[half]
+            rows[j] = (mine ^ offset(CALLS[call][0] + i)) * (2 * units) + columns[half]
         for k in range(units):
             for j in live:
                 call, half = lists[j]
                 list_ref[found[j]] = (place(CALLS[call][0] + i) * units + k) * SHIFT + i * units + k
                 found[j] = found[j] + mask_ref[rows[j] + 2 * k]
     for j in range(len(lists)):
-        count_ref[j] = found[j] - j * stride
-
-
-def pair_kernel(count_ref, list_ref, nod_ref, ctl_ref, before_ref, part_ref, csum_ref, node_ref, acc_ref, *, call, stride, part):
+        list_ref[len(lists) * stride + j] = found[j] - j * stride
+
+
+def pair_kernel(list_ref, nod_ref, ctl_ref, before_ref, part_ref, csum_ref, node_ref, acc_ref, *, call, stride, part):
     node_ref[...] = jnp.zeros_like(node_ref)
     acc_ref[...] = jnp.zeros_like(acc_ref)
     for half in range(2):
@@ -101,14 +102,14 @@
             body(i, 1)
             return 0
 
-        count = count_ref[row]
+        count = list_ref[2 * len(CALLS) * stride + row]
         lax.fori_loop(0, count // GROUP, group, 0)
         lax.fori_loop(count // GROUP * GROUP, count, single, 0)
     part_ref[...] = node_ref[:, : part_ref.shape[1], :]
     for k in range(6):
         for s in range(0, acc_ref.shape[1], TILE):
             total = jnp.sum(acc_ref[k, pl.ds(s, TILE), :].T, axis=0, keepdims=True)
-            csum_ref[pl.ds(k, 1), pl.ds(s, TILE)] = before_ref[pl.ds(k, 1), pl.ds(s, TILE)] + total
+            csum_ref[k, :, pl.ds(s, TILE)] = before_ref[k, :, pl.ds(s, TILE)] + total
 
 
 def local(node_points, cotangent, ctl_points, ctl_weights, tile_mask):
@@ -124,48 +125,44 @@
     vmem = pl.BlockSpec(memory_space=pltpu.VMEM)
     smem = pl.BlockSpec(memory_space=pltpu.SMEM)
     stride = max(blocks for _, blocks in CALLS) * units + 8
-    where = jnp.stack([lax.axis_index("ctl"), lax.axis_index("vol") * part // TILE]).astype(jnp.int32)
     mask = tile_mask.reshape(2 * tiles)
 
     nod = jnp.concatenate([node_points, cotangent], axis=0).reshape(6, units, TILE)
-    ctl = jnp.concatenate([ctl_points, ctl_weights], axis=0).reshape(6, part)
+    ctl = jnp.concatenate([ctl_points, ctl_weights], axis=0)
     for step, (node_bit, ctl_bit) in enumerate(zip(NODE_BITS, CTL_BITS)):
         nod_new = swap(nod, "ctl", node_bit)
         ctl_new = swap(ctl, "vol", ctl_bit)
         if step == 1:
-            nod_new, where, mask = lax.optimization_barrier((nod_new, where, mask))
+            nod_new, mask = lax.optimization_barrier((nod_new, mask))
         if step == 2:
-            lists, counts = pl.pallas_call(
-                functools.partial(list_kernel, units=units, stride=stride),
-                out_shape=(
-                    jax.ShapeDtypeStruct((2 * len(CALLS) * stride,), jnp.int32),
-                    jax.ShapeDtypeStruct((2 * len(CALLS),), jnp.int32),
-                ),
-                in_specs=[smem, smem],
-                out_specs=(smem, smem),
+            lists = pl.pallas_call(
+                functools.partial(list_kernel, units=units, stride=stride, tall=TILE // part),
+                out_shape=jax.ShapeDtypeStruct((2 * len(CALLS) * (stride + 1),), jnp.int32),
+                in_specs=[smem],
+                out_specs=smem,
                 name="kept_tiles",
-            )(where, mask)
-            nod_new, lists, counts = lax.optimization_barrier((nod_new, lists, counts))
+            )(mask)
+            nod_new, lists = lax.optimization_barrier((nod_new, lists))
         nod = jnp.concatenate([nod, nod_new], axis=1)
-        ctl = jnp.concatenate([ctl, ctl_new], axis=1)
+        ctl = jnp.concatenate([ctl, ctl_new], axis=2)
     nod = jnp.pad(nod, ((0, 0), (0, 8), (0, 0)))
-    ctl = jnp.broadcast_to(ctl[:, :, None], (6, width, TILE))
+    ctl = jnp.broadcast_to(ctl.reshape(6, width, 1), (6, width, TILE))
 
     def pairs(call, csum):
         rows = CALLS[call][1] * units
         work = rows * TILE * width
         return pl.pallas_call(
             functools.partial(pair_kernel, call=call, stride=stride, part=part),
-            out_shape=(jax.ShapeDtypeStruct((3, rows, TILE), f32), jax.ShapeDtypeStruct((6, width), f32)),
-            in_specs=[smem, smem, vmem, vmem, vmem],
+            out_shape=(jax.ShapeDtypeStruct((3, rows, TILE), f32), jax.ShapeDtypeStruct((6, 1, width), f32)),
+            in_specs=[smem, vmem, vmem, vmem],
             out_specs=(vmem, vmem),
             scratch_shapes=[pltpu.VMEM((3, rows + 8, TILE), f32), pltpu.VMEM((6, width, TILE), f32)],
             compiler_params=pltpu.CompilerParams(vmem_limit_bytes=32 << 20),
             cost_estimate=pl.CostEstimate(flops=5000 * work, bytes_accessed=16 * work, transcendentals=work),
             name="pairs",
-        )(counts, lists, nod, ctl, csum)
-
-    mine, csum = pairs(0, jnp.zeros((6, width), f32))
+        )(lists, nod, ctl, csum)
+
+    mine, csum = pairs(0, jnp.zeros((6, 1, width), f32))
     got = []
     for step in range(1, len(CALLS)):
         got = [g[:, g.shape[1] // 2 :] for g in got], [g[:, : g.shape[1] // 2] for g in got]
@@ -177,8 +174,8 @@
     ckeep = csum
     sent = []
     for step, bit in enumerate(CTL_BITS[::-1]):
-        span = ckeep.shape[1] // 2
-        csend = swap(ckeep[:, span:], "vol", bit)
+        span = ckeep.shape[2] // 2
+        csend = swap(ckeep[:, :, span:], "vol", bit)
         if sent:
             if step < len(CTL_BITS) - 1:
                 csend, *sent = lax.optimization_barrier((csend, *sent))
@@ -188,13 +185,13 @@
             size = keep.shape[1] // 2
             sent = [keep[:, :size], swap(keep[:, size:], "ctl", SUM_BITS[len(CALLS) - 1 + step])]
         if step < len(CTL_BITS) - 1:
-            ckeep = ckeep[:, :span] + csend
+            ckeep = ckeep[:, :, :span] + csend
     if sent:
         keep = sent[0] + sent[1]
     node_grad = keep.reshape(3, 1, own) * (-20.0 / math.sqrt(total_ctl))
-    ckeep = ckeep[:, :span] + csend
-    weight_grad = ckeep[:3].reshape(3, 1, part) * (4.0 / math.sqrt(total_nodes))
-    control_grad = ckeep[3:].reshape(3, 1, part) * (20.0 / math.sqrt(total_nodes))
+    ckeep = ckeep[:, :, :span] + csend
+    weight_grad = ckeep[:3] * (4.0 / math.sqrt(total_nodes))
+    control_grad = ckeep[3:] * (20.0 / math.sqrt(total_nodes))
     return (node_grad, weight_grad, control_grad)
 
 

time: 89 us -> 87.5 us (0.983)
  waiting for transfers between devices: 14.8 us -> 11.4 us
  starting transfers between devices: 29.7 us -> 32.1 us
  local copies, waits for them, and re-layouts: 3.42 us -> 2.3 us
    ppermute x16, waiting for transfers between devices: 14.8 us -> 11.4 us  [swap(): lax.ppermute(value, axis, [(i, i ^ bit) for i in range(lax.axis_size(axis...]
    ppermute x16, starting transfers between devices: 29.7 us -> 32.1 us  [swap(): lax.ppermute(value, axis, [(i, i ^ bit) for i in range(lax.axis_size(axis...]
    unnamed x19 -> x15, local copies, waits for them, and re-layouts: 2.01 us -> 0.86 us
  transfers between devices with their start and end apart: 16 -> 16, of which waited for: 6 -> 6; matrix products, arithmetic and copies ran while one was open for 4% -> 2% of each run, Pallas kernels for 22% -> 23%
where the time goes in v4:
time: 87.5 us; the launch traced here: 86.2 us
  Pallas kernels  37.3 us (43%)
  starting transfers between devices  32.1 us (37%)
  waiting for transfers between devices  11.4 us (13%)
  other arithmetic  2.35 us (3%)
  local copies, waits for them, and re-layouts  2.3 us (3%)
  between operations  0.89 us (1%)
    pallas_call x2, Pallas kernels, pairs(): pl.pallas_call(functools.partial(pair_kernel, call=call, stride=stride, p...  35 us
    ppermute x16, starting transfers between devices, swap(): lax.ppermute(value, axis, [(i, i ^ bit) for i in range(lax.axis_size(axis...  32.1 us
    ppermute x16, waiting for transfers between devices, swap(): lax.ppermute(value, axis, [(i, i ^ bit) for i in range(lax.axis_size(axis...  11.4 us
    pallas_call x1, Pallas kernels, local(): pl.pallas_call(functools.partial(list_kernel, units=units, stride=stride,...  2.24 us
  transfers between devices with their start and end apart: 16, of which 6 were waited for; matrix products, arithmetic and copies ran while one was open for 2% of the time, Pallas kernels for 23%

profile of v4, /device:TPU:2, one launch (start us, length us, event | category | flops | bytes accessed | tf_op | source)
XLA Modules:
  0.0 86.2 jit_solution(10985182379511538224)
XLA Ops:
  0.6 0.8 pad_maximum_fusion.3
  1.4 0.0 copy-start.2
  1.4 0.0 copy-start.3
  1.5 1.6 %collective-permute-start = (f32[6,16,128]{2,1,0:T(8,128)S(1)}, f32[6,16,128]{2,1,0:T(8,128)S(1)}, u32[]{:S(2)}, u32[]{:S(2)}) collective-permute-start(f32[6,16,128]{2,1,0:T(8,128)S(1)} %bitcast.9), channel_id=1, source_target_pairs={{0,12},{1,13},{2,14},{3,15},{4,8},{5,9},{6,10},{7,11},{8,4},{9,5},... | collective-permute-start | bytes 147464 | tf_op jit(solution)/shard_map/ppermute | solution.py:34
  3.0 0.0 copy-done.2
  3.0 0.0 copy-done.3
  3.0 0.0 copy-start.1
  3.1 6.4 %collective-permute-start.4 = (f32[6,1,16]{2,1,0:T(1,128)S(1)}, f32[6,1,16]{2,1,0:T(1,128)S(1)}, u32[]{:S(2)}, u32[]{:S(2)}) collective-permute-start(f32[6,1,16]{2,1,0:T(1,128)S(1)} %constant_dynamic-update-slice_fusion.5), channel_id=1, source_target_pairs={{0,192},{16,208},{32,224},{48,240},{64,128},{80,144},{96,160},{112... | collective-permute-start | bytes 1160 | tf_op jit(solution)/shard_map/ppermute | solution.py:34
  9.5 0.0 copy-done.1
  9.5 0.1 copy.9
  9.6 0.7 reshape.30.mask_ref
  10.3 0.0 collective-permute-done
  10.3 3.3 %collective-permute-start.1 = (f32[6,32,128]{2,1,0:T(8,128)S(1)}, f32[6,32,128]{2,1,0:T(8,128)S(1)}, u32[]{:S(2)}, u32[]{:S(2)}) collective-permute-start(f32[6,32,128]{2,1,0:T(8,128)S(1)} %pad_maximum_fusion.2), channel_id=1, source_target_pairs={{0,2},{1,3},{2,0},{3,1},{4,6},{5,7},{6,4},{7,5},{8,10},{9,11},{10,... | collective-permute-start | bytes 294920 | tf_op jit(solution)/shard_map/ppermute | solution.py:34
  13.6 0.0 collective-permute-done.4
  13.6 0.1 pad_maximum_fusion.4
  13.7 1.5 %collective-permute-start.5 = (f32[6,1,32]{2,1,0:T(1,128)S(1)}, f32[6,1,32]{2,1,0:T(1,128)S(1)}, u32[]{:S(2)}, u32[]{:S(2)}) collective-permute-start(f32[6,1,32]{2,1,0:T(1,128)S(1)} %pad_maximum_fusion.4), channel_id=1, source_target_pairs={{0,64},{16,80},{32,96},{48,112},{64,0},{80,16},{96,32},{112,48},{1... | collective-permute-start | bytes 2312 | tf_op jit(solution)/shard_map/ppermute | solution.py:34
  15.2 1.4 %collective-permute-done.1 = f32[6,32,128]{2,1,0:T(8,128)S(1)} collective-permute-done((f32[6,32,128]{2,1,0:T(8,128)S(1)}, f32[6,32,128]{2,1,0:T(8,128)S(1)}, u32[]{:S(2)}, u32[]{:S(2)}) %collective-permute-start.1) | collective-permute-done | bytes 98336 | tf_op jit(solution)/shard_map/ppermute | solution.py:34
  16.5 1.9 %collective-permute-start.2 = (f32[6,64,128]{2,1,0:T(8,128)S(1)}, f32[6,64,128]{2,1,0:T(8,128)S(1)}, u32[]{:S(2)}, u32[]{:S(2)}) collective-permute-start(f32[6,64,128]{2,1,0:T(8,128)S(1)} %pad_maximum_fusion.1), channel_id=1, source_target_pairs={{0,4},{1,5},{2,6},{3,7},{4,0},{5,1},{6,2},{7,3},{8,12},{9,13},{10,... | collective-permute-start | bytes 589832 | tf_op jit(solution)/shard_map/ppermute | solution.py:34
  18.4 0.0 collective-permute-done.5
  18.4 0.1 pad_maximum_fusion.5
  18.5 1.1 %collective-permute-start.6 = (f32[6,1,64]{2,1,0:T(1,128)S(1)}, f32[6,1,64]{2,1,0:T(1,128)S(1)}, u32[]{:S(2)}, u32[]{:S(2)}) collective-permute-start(f32[6,1,64]{2,1,0:T(1,128)S(1)} %pad_maximum_fusion.5), channel_id=1, source_target_pairs={{0,32},{16,48},{32,0},{48,16},{64,96},{80,112},{96,64},{112,80},{1... | collective-permute-start | bytes 4616 | tf_op jit(solution)/shard_map/ppermute | solution.py:34
  19.6 2.6 %collective-permute-done.6 = f32[6,1,64]{2,1,0:T(1,128)S(1)} collective-permute-done((f32[6,1,64]{2,1,0:T(1,128)S(1)}, f32[6,1,64]{2,1,0:T(1,128)S(1)}, u32[]{:S(2)}, u32[]{:S(2)}) %collective-permute-start.6) | collective-permute-done | bytes 1568 | tf_op jit(solution)/shard_map/ppermute | solution.py:34
  22.2 0.1 pad_maximum_fusion.6
  22.2 1.7 %collective-permute-start.7 = (f32[6,1,128]{2,1,0:T(1,128)S(1)}, f32[6,1,128]{2,1,0:T(1,128)S(1)}, u32[]{:S(2)}, u32[]{:S(2)}) collective-permute-start(f32[6,1,128]{2,1,0:T(1,128)S(1)} %pad_maximum_fusion.6), channel_id=1, source_target_pairs={{0,16},{16,0},{32,48},{48,32},{64,80},{80,64},{96,112},{112,96},{1... | collective-permute-start | bytes 9224 | tf_op jit(solution)/shard_map/ppermute | solution.py:34
  23.9 2.2 %kept_tiles.1.list_ref = s32[548]{0:T(1024)} custom-call(s32[512]{0:T(512)} %reshape.30.mask_ref), custom_call_target="tpu_custom_call" | custom-call | tf_op jit(solution)/shard_map/kept_tiles/pallas_call | solution.py:138
  26.2 0.0 collective-permute-done.2
  26.2 0.1 collective-permute-start.3
  26.3 0.0 collective-permute-done.7
  26.3 0.1 concatenate.45
  26.5 1.5 %collective-permute-done.3 = f32[6,128,128]{2,1,0:T(8,128)S(1)} collective-permute-done((f32[6,128,128]{2,1,0:T(8,128)S(1)}, f32[6,128,128]{2,1,0:T(8,128)S(1)}, u32[]{:S(2)}, u32[]{:S(2)}) %collective-permute-start.3) | collective-permute-done | bytes 393248 | tf_op jit(solution)/shard_map/ppermute | solution.py:34
  28.1 0.1 pad.4.nod_ref
  28.1 0.3 broadcast_in_dim.11.ctl_ref
  28.4 0.0 copy-start
  28.4 0.7 copy-done
  29.1 17.3 %pairs.2 = (f32[3,128,128]{2,1,0:T(8,128)S(1)}, f32[6,1,256]{2,1,0:T(1,128)S(1)}) custom-call(s32[548]{0:T(1024)S(1)} %copy-done, f32[6,264,128]{2,1,0:T(8,128)S(1)} %pad.4.nod_ref, f32[6,256,128]{2,1,0:T(8,128)S(1)} %broadcast_in_dim.11.ctl_ref, f32[6,1,256]{2,1,0:T(1,128)S(1)} %broadcast_in_dim.12.before_ref), custom_call_target="tpu_custom_call" | custom-call | flops 20971520000 | bytes 67108864 | tf_op jit(solution)/shard_map/pairs/pallas_call | solution.py:154
  46.4 0.1 collective-permute-start.8
  46.5 17.7 %pairs.3 = (f32[3,128,128]{2,1,0:T(8,128)S(1)}, f32[6,1,256]{2,1,0:T(1,128)S(1)}) custom-call(s32[548]{0:T(1024)S(1)} %copy-done, f32[6,264,128]{2,1,0:T(8,128)S(1)} %pad.4.nod_ref, f32[6,256,128]{2,1,0:T(8,128)S(1)} %broadcast_in_dim.11.ctl_ref, f32[6,1,256]{2,1,0:T(1,128)S(1)} %get-tuple-element.23.before_ref), custom_call_target="tpu_custom_call" | custom-call | flops 20971520000 | bytes 67108864 | tf_op jit(solution)/shard_map/pairs/pallas_call | solution.py:154
  64.2 0.0 collective-permute-done.8
  64.2 1.7 %collective-permute-start.9 = (f32[6,1,128]{2,1,0:T(1,128)S(1)}, f32[6,1,128]{2,1,0:T(1,128)S(1)}, u32[]{:S(2)}, u32[]{:S(2)}) collective-permute-start(f32[6,1,128]{2,1,0:T(1,128)S(1)} %slice.49), channel_id=1, source_target_pairs={{0,16},{16,0},{32,48},{48,32},{64,80},{80,64},{96,112},{112,96},{1... | collective-permute-start | bytes 9224 | tf_op jit(solution)/shard_map/ppermute | solution.py:34
  65.9 4.0 %collective-permute-start.11 = (f32[3,64,128]{2,1,0:T(8,128)S(1)}, f32[3,64,128]{2,1,0:T(8,128)S(1)}, u32[]{:S(2)}, u32[]{:S(2)}) collective-permute-start(f32[3,64,128]{2,1,0:T(8,128)S(1)} %get-tuple-element.41), channel_id=1, source_target_pairs={{0,2},{1,3},{2,0},{3,1},{4,6},{5,7},{6,4},{7,5},{8,10},{9,11},{10,... | collective-permute-start | bytes 294920 | tf_op jit(solution)/shard_map/ppermute | solution.py:34
  70.0 0.0 collective-permute-done.9
  70.0 0.1 slice.65
  70.1 1.4 %collective-permute-start.10 = (f32[6,1,64]{2,1,0:T(1,128)S(1)}, f32[6,1,64]{2,1,0:T(1,128)S(1)}, u32[]{:S(2)}, u32[]{:S(2)}) collective-permute-start(f32[6,1,64]{2,1,0:T(1,128)S(1)} %slice.65), channel_id=1, source_target_pairs={{0,32},{16,48},{32,0},{48,16},{64,96},{80,112},{96,64},{112,80},{1... | collective-permute-start | bytes 4616 | tf_op jit(solution)/shard_map/ppermute | solution.py:34
  71.5 2.2 %collective-permute-done.10 = f32[6,1,64]{2,1,0:T(1,128)S(1)} collective-permute-done((f32[6,1,64]{2,1,0:T(1,128)S(1)}, f32[6,1,64]{2,1,0:T(1,128)S(1)}, u32[]{:S(2)}, u32[]{:S(2)}) %collective-permute-start.10) | collective-permute-done | bytes 1568 | tf_op jit(solution)/shard_map/ppermute | solution.py:34
  73.7 0.0 collective-permute-done.11
  73.7 0.9 %collective-permute-start.13 = (f32[3,32,128]{2,1,0:T(8,128)S(1)}, f32[3,32,128]{2,1,0:T(8,128)S(1)}, u32[]{:S(2)}, u32[]{:S(2)}) collective-permute-start(f32[3,32,128]{2,1,0:T(8,128)S(1)} %get-tuple-element.43), channel_id=1, source_target_pairs={{0,4},{1,5},{2,6},{3,7},{4,0},{5,1},{6,2},{7,3},{8,12},{9,13},{10,... | collective-permute-start | bytes 147464 | tf_op jit(solution)/shard_map/ppermute | solution.py:34
  74.6 0.1 slice.68
  74.7 2.4 %collective-permute-start.12 = (f32[6,1,32]{2,1,0:T(1,128)S(1)}, f32[6,1,32]{2,1,0:T(1,128)S(1)}, u32[]{:S(2)}, u32[]{:S(2)}) collective-permute-start(f32[6,1,32]{2,1,0:T(1,128)S(1)} %slice.68), channel_id=1, source_target_pairs={{0,64},{16,80},{32,96},{48,112},{64,0},{80,16},{96,32},{112,48},{1... | collective-permute-start | bytes 2312 | tf_op jit(solution)/shard_map/ppermute | solution.py:34
  77.1 2.1 %collective-permute-done.12 = f32[6,1,32]{2,1,0:T(1,128)S(1)} collective-permute-done((f32[6,1,32]{2,1,0:T(1,128)S(1)}, f32[6,1,32]{2,1,0:T(1,128)S(1)}, u32[]{:S(2)}, u32[]{:S(2)}) %collective-permute-start.12) | collective-permute-done | bytes 800 | tf_op jit(solution)/shard_map/ppermute | solution.py:34
  79.2 0.0 collective-permute-done.13
  79.2 0.1 slice.75
  79.3 4.0 %collective-permute-start.15 = (f32[6,1,16]{2,1,0:T(1,128)S(1)}, f32[6,1,16]{2,1,0:T(1,128)S(1)}, u32[]{:S(2)}, u32[]{:S(2)}) collective-permute-start(f32[6,1,16]{2,1,0:T(1,128)S(1)} %slice.75), channel_id=1, source_target_pairs={{0,192},{16,208},{32,224},{48,240},{64,128},{80,144},{96,160},{112... | collective-permute-start | bytes 1160 | tf_op jit(solution)/shard_map/ppermute | solution.py:34
  83.3 0.1 collective-permute-start.14
  83.4 1.6 %collective-permute-done.15 = f32[6,1,16]{2,1,0:T(1,128)S(1)} collective-permute-done((f32[6,1,16]{2,1,0:T(1,128)S(1)}, f32[6,1,16]{2,1,0:T(1,128)S(1)}, u32[]{:S(2)}, u32[]{:S(2)}) %collective-permute-start.15) | collective-permute-done | bytes 416 | tf_op jit(solution)/shard_map/ppermute | solution.py:34
  85.0 0.6 slice_multiply_fusion
  85.6 0.0 collective-permute-done.14
  85.6 0.6 fusion
  (23 shorter events, 0.2 us)
Async XLA Ops:
  1.4 1.6 %copy-start.2 = (f32[3,1,16]{2,1,0:T(1,128)S(1)}, f32[3,1,16]{2,1,0:T(1,128)}, u32[]{:S(2)}) copy-start(f32[3,1,16]{2,1,0:T(1,128)} %param.7) | copy-start | bytes 580
  1.4 1.6 %copy-start.3 = (f32[3,1,16]{2,1,0:T(1,128)S(1)}, f32[3,1,16]{2,1,0:T(1,128)}, u32[]{:S(2)}) copy-start(f32[3,1,16]{2,1,0:T(1,128)} %param.8) | copy-start | bytes 580
  1.5 8.8 %collective-permute-start = (f32[6,16,128]{2,1,0:T(8,128)S(1)}, f32[6,16,128]{2,1,0:T(8,128)S(1)}, u32[]{:S(2)}, u32[]{:S(2)}) collective-permute-start(f32[6,16,128]{2,1,0:T(8,128)S(1)} %bitcast.9), channel_id=1, source_target_pairs={{0,12},{1,13},{2,14},{3,15},{4,8},{5,9},{6,10},{7,11},{8,4},{9,5},... | collective-permute-start | bytes 147464 | tf_op jit(solution)/shard_map/ppermute | solution.py:34
  3.0 6.4 %copy-start.1 = (s32[1,256,1,2]{1,3,2,0:T(2,128)S(1)}, s32[1,256,1,2]{1,3,2,0:T(2,128)}, u32[]{:S(2)}) copy-start(s32[1,256,1,2]{1,3,2,0:T(2,128)} %param.9) | copy-start | bytes 6148
  3.1 10.5 %collective-permute-start.4 = (f32[6,1,16]{2,1,0:T(1,128)S(1)}, f32[6,1,16]{2,1,0:T(1,128)S(1)}, u32[]{:S(2)}, u32[]{:S(2)}) collective-permute-start(f32[6,1,16]{2,1,0:T(1,128)S(1)} %constant_dynamic-update-slice_fusion.5), channel_id=1, source_target_pairs={{0,192},{16,208},{32,224},{48,240},{64,128},{80,144},{96,160},{112... | collective-permute-start | bytes 1160 | tf_op jit(solution)/shard_map/ppermute | solution.py:34
  10.3 6.2 %collective-permute-start.1 = (f32[6,32,128]{2,1,0:T(8,128)S(1)}, f32[6,32,128]{2,1,0:T(8,128)S(1)}, u32[]{:S(2)}, u32[]{:S(2)}) collective-permute-start(f32[6,32,128]{2,1,0:T(8,128)S(1)} %pad_maximum_fusion.2), channel_id=1, source_target_pairs={{0,2},{1,3},{2,0},{3,1},{4,6},{5,7},{6,4},{7,5},{8,10},{9,11},{10,... | collective-permute-start | bytes 294920 | tf_op jit(solution)/shard_map/ppermute | solution.py:34
  13.7 4.8 %collective-permute-start.5 = (f32[6,1,32]{2,1,0:T(1,128)S(1)}, f32[6,1,32]{2,1,0:T(1,128)S(1)}, u32[]{:S(2)}, u32[]{:S(2)}) collective-permute-start(f32[6,1,32]{2,1,0:T(1,128)S(1)} %pad_maximum_fusion.4), channel_id=1, source_target_pairs={{0,64},{16,80},{32,96},{48,112},{64,0},{80,16},{96,32},{112,48},{1... | collective-permute-start | bytes 2312 | tf_op jit(solution)/shard_map/ppermute | solution.py:34
  16.5 9.6 %collective-permute-start.2 = (f32[6,64,128]{2,1,0:T(8,128)S(1)}, f32[6,64,128]{2,1,0:T(8,128)S(1)}, u32[]{:S(2)}, u32[]{:S(2)}) collective-permute-start(f32[6,64,128]{2,1,0:T(8,128)S(1)} %pad_maximum_fusion.1), channel_id=1, source_target_pairs={{0,4},{1,5},{2,6},{3,7},{4,0},{5,1},{6,2},{7,3},{8,12},{9,13},{10,... | collective-permute-start | bytes 589832 | tf_op jit(solution)/shard_map/ppermute | solution.py:34
  18.5 3.6 %collective-permute-start.6 = (f32[6,1,64]{2,1,0:T(1,128)S(1)}, f32[6,1,64]{2,1,0:T(1,128)S(1)}, u32[]{:S(2)}, u32[]{:S(2)}) collective-permute-start(f32[6,1,64]{2,1,0:T(1,128)S(1)} %pad_maximum_fusion.5), channel_id=1, source_target_pairs={{0,32},{16,48},{32,0},{48,16},{64,96},{80,112},{96,64},{112,80},{1... | collective-permute-start | bytes 4616 | tf_op jit(solution)/shard_map/ppermute | solution.py:34
  22.2 4.1 %collective-permute-start.7 = (f32[6,1,128]{2,1,0:T(1,128)S(1)}, f32[6,1,128]{2,1,0:T(1,128)S(1)}, u32[]{:S(2)}, u32[]{:S(2)}) collective-permute-start(f32[6,1,128]{2,1,0:T(1,128)S(1)} %pad_maximum_fusion.6), channel_id=1, source_target_pairs={{0,16},{16,0},{32,48},{48,32},{64,80},{80,64},{96,112},{112,96},{1... | collective-permute-start | bytes 9224 | tf_op jit(solution)/shard_map/ppermute | solution.py:34
  26.2 1.8 %collective-permute-start.3 = (f32[6,128,128]{2,1,0:T(8,128)S(1)}, f32[6,128,128]{2,1,0:T(8,128)S(1)}, u32[]{:S(2)}, u32[]{:S(2)}) collective-permute-start(f32[6,128,128]{2,1,0:T(8,128)S(1)} %pad_maximum_fusion), channel_id=1, source_target_pairs={{0,1},{1,0},{2,3},{3,2},{4,5},{5,4},{6,7},{7,6},{8,9},{9,8},{10,11... | collective-permute-start | bytes 1179656 | tf_op jit(solution)/shard_map/ppermute | solution.py:34
  28.4 0.7 copy-start
  46.4 17.8 %collective-permute-start.8 = (f32[3,128,128]{2,1,0:T(8,128)S(1)}, f32[3,128,128]{2,1,0:T(8,128)S(1)}, u32[]{:S(2)}, u32[]{:S(2)}) collective-permute-start(f32[3,128,128]{2,1,0:T(8,128)S(1)} %get-tuple-element.25), channel_id=1, source_target_pairs={{0,12},{1,13},{2,14},{3,15},{4,8},{5,9},{6,10},{7,11},{8,4},{9,5},... | collective-permute-start | bytes 589832 | tf_op jit(solution)/shard_map/ppermute | solution.py:34
  64.2 5.7 %collective-permute-start.9 = (f32[6,1,128]{2,1,0:T(1,128)S(1)}, f32[6,1,128]{2,1,0:T(1,128)S(1)}, u32[]{:S(2)}, u32[]{:S(2)}) collective-permute-start(f32[6,1,128]{2,1,0:T(1,128)S(1)} %slice.49), channel_id=1, source_target_pairs={{0,16},{16,0},{32,48},{48,32},{64,80},{80,64},{96,112},{112,96},{1... | collective-permute-start | bytes 9224 | tf_op jit(solution)/shard_map/ppermute | solution.py:34
  65.9 7.7 %collective-permute-start.11 = (f32[3,64,128]{2,1,0:T(8,128)S(1)}, f32[3,64,128]{2,1,0:T(8,128)S(1)}, u32[]{:S(2)}, u32[]{:S(2)}) collective-permute-start(f32[3,64,128]{2,1,0:T(8,128)S(1)} %get-tuple-element.41), channel_id=1, source_target_pairs={{0,2},{1,3},{2,0},{3,1},{4,6},{5,7},{6,4},{7,5},{8,10},{9,11},{10,... | collective-permute-start | bytes 294920 | tf_op jit(solution)/shard_map/ppermute | solution.py:34
  70.1 3.6 %collective-permute-start.10 = (f32[6,1,64]{2,1,0:T(1,128)S(1)}, f32[6,1,64]{2,1,0:T(1,128)S(1)}, u32[]{:S(2)}, u32[]{:S(2)}) collective-permute-start(f32[6,1,64]{2,1,0:T(1,128)S(1)} %slice.65), channel_id=1, source_target_pairs={{0,32},{16,48},{32,0},{48,16},{64,96},{80,112},{96,64},{112,80},{1... | collective-permute-start | bytes 4616 | tf_op jit(solution)/shard_map/ppermute | solution.py:34
  73.7 5.5 %collective-permute-start.13 = (f32[3,32,128]{2,1,0:T(8,128)S(1)}, f32[3,32,128]{2,1,0:T(8,128)S(1)}, u32[]{:S(2)}, u32[]{:S(2)}) collective-permute-start(f32[3,32,128]{2,1,0:T(8,128)S(1)} %get-tuple-element.43), channel_id=1, source_target_pairs={{0,4},{1,5},{2,6},{3,7},{4,0},{5,1},{6,2},{7,3},{8,12},{9,13},{10,... | collective-permute-start | bytes 147464 | tf_op jit(solution)/shard_map/ppermute | solution.py:34
  74.7 4.5 %collective-permute-start.12 = (f32[6,1,32]{2,1,0:T(1,128)S(1)}, f32[6,1,32]{2,1,0:T(1,128)S(1)}, u32[]{:S(2)}, u32[]{:S(2)}) collective-permute-start(f32[6,1,32]{2,1,0:T(1,128)S(1)} %slice.68), channel_id=1, source_target_pairs={{0,64},{16,80},{32,96},{48,112},{64,0},{80,16},{96,32},{112,48},{1... | collective-permute-start | bytes 2312 | tf_op jit(solution)/shard_map/ppermute | solution.py:34
  79.3 5.7 %collective-permute-start.15 = (f32[6,1,16]{2,1,0:T(1,128)S(1)}, f32[6,1,16]{2,1,0:T(1,128)S(1)}, u32[]{:S(2)}, u32[]{:S(2)}) collective-permute-start(f32[6,1,16]{2,1,0:T(1,128)S(1)} %slice.75), channel_id=1, source_target_pairs={{0,192},{16,208},{32,224},{48,240},{64,128},{80,144},{96,160},{112... | collective-permute-start | bytes 1160 | tf_op jit(solution)/shard_map/ppermute | solution.py:34
  83.3 2.3 %collective-permute-start.14 = (f32[3,16,128]{2,1,0:T(8,128)S(1)}, f32[3,16,128]{2,1,0:T(8,128)S(1)}, u32[]{:S(2)}, u32[]{:S(2)}) collective-permute-start(f32[3,16,128]{2,1,0:T(8,128)S(1)} %slice.72), channel_id=1, source_target_pairs={{0,1},{1,0},{2,3},{3,2},{4,5},{5,4},{6,7},{7,6},{8,9},{9,8},{10,11... | collective-permute-start | bytes 73736 | tf_op jit(solution)/shard_map/ppermute | solution.py:34

commit v5 on v4

--- a/solution.py
+++ b/solution.py
@@ -44,12 +44,13 @@
         rows = {}
         for j in live:
             call, half = lists[j]
-            rows[j] = (mine ^ offset(CALLS[call][0] + i)) * (2 * units) + columns[half]
+            row = (mine ^ offset(CALLS[call][0] + i)) * units
+            rows[j] = (row // TILE, columns[half], row % TILE)
         for k in range(units):
             for j in live:
                 call, half = lists[j]
                 list_ref[found[j]] = (place(CALLS[call][0] + i) * units + k) * SHIFT + i * units + k
-                found[j] = found[j] + mask_ref[rows[j] + 2 * k]
+                found[j] = found[j] + mask_ref[rows[j][0], rows[j][1], rows[j][2] + k]
     for j in range(len(lists)):
         list_ref[len(lists) * stride + j] = found[j] - j * stride
 
@@ -125,7 +126,7 @@
     vmem = pl.BlockSpec(memory_space=pltpu.VMEM)
     smem = pl.BlockSpec(memory_space=pltpu.SMEM)
     stride = max(blocks for _, blocks in CALLS) * units + 8
-    mask = tile_mask.reshape(2 * tiles)
+    mask = tile_mask.reshape(tiles, 2).T.reshape(2, tiles // TILE, TILE).transpose(1, 0, 2)
 
     nod = jnp.concatenate([node_points, cotangent], axis=0).reshape(6, units, TILE)
     ctl = jnp.concatenate([ctl_points, ctl_weights], axis=0)

time: 87.5 us -> 88.4 us (1.010); the launches traced: 86.2 us -> 88.6 us
  waiting for transfers between devices: 11.4 us -> 14.9 us
  starting transfers between devices: 32.1 us -> 29.9 us
  Pallas kernels: 37.3 us -> 39.1 us
    ppermute x16, waiting for transfers between devices: 11.4 us -> 14.9 us  [swap(): lax.ppermute(value, axis, [(i, i ^ bit) for i in range(lax.axis_size(axis...]
    ppermute x16, starting transfers between devices: 32.1 us -> 29.9 us  [swap(): lax.ppermute(value, axis, [(i, i ^ bit) for i in range(lax.axis_size(axis...]
    pallas_call x2, Pallas kernels: 35 us -> 36 us  [pairs(): pl.pallas_call(functools.partial(pair_kernel, call=call, stride=stride, p...]
  transfers between devices with their start and end apart: 16 -> 16, of which waited for: 6 -> 6; matrix products, arithmetic and copies ran while one was open for 2% -> 1% of each run, Pallas kernels for 23% -> 23%
where the time goes in v5:
time: 88.4 us; the launch traced here: 88.6 us
  Pallas kernels  39.1 us (44%)
  starting transfers between devices  29.9 us (34%)
  waiting for transfers between devices  14.9 us (17%)
  other arithmetic  2.35 us (3%)
  local copies, waits for them, and re-layouts  1.46 us (2%)
    pallas_call x2, Pallas kernels, pairs(): pl.pallas_call(functools.partial(pair_kernel, call=call, stride=stride, p...  36 us
    ppermute x16, starting transfers between devices, swap(): lax.ppermute(value, axis, [(i, i ^ bit) for i in range(lax.axis_size(axis...  29.9 us
    ppermute x16, waiting for transfers between devices, swap(): lax.ppermute(value, axis, [(i, i ^ bit) for i in range(lax.axis_size(axis...  14.9 us
    pallas_call x1, Pallas kernels, local(): pl.pallas_call(functools.partial(list_kernel, units=units, stride=stride,...  3.04 us
  transfers between devices with their start and end apart: 16, of which 6 were waited for; matrix products, arithmetic and copies ran while one was open for 1% of the time, Pallas kernels for 23%

profile of v5, /device:TPU:2, one launch (start us, length us, event | category | flops | bytes accessed | tf_op | source)
XLA Modules:
  0.0 88.6 jit_solution(17874891530972156947)
XLA Ops:
  0.6 0.8 pad_maximum_fusion.3
  1.4 0.0 copy-start.1
  1.4 0.0 copy-start.2
  1.5 1.6 %collective-permute-start = (f32[6,16,128]{2,1,0:T(8,128)S(1)}, f32[6,16,128]{2,1,0:T(8,128)S(1)}, u32[]{:S(2)}, u32[]{:S(2)}) collective-permute-start(f32[6,16,128]{2,1,0:T(8,128)S(1)} %bitcast.12), channel_id=1, source_target_pairs={{0,12},{1,13},{2,14},{3,15},{4,8},{5,9},{6,10},{7,11},{8,4},{9,5},... | collective-permute-start | bytes 147464 | tf_op jit(solution)/shard_map/ppermute | solution.py:34
  3.0 0.0 copy-done.1
  3.0 0.0 copy-done.2
  3.1 6.4 %collective-permute-start.4 = (f32[6,1,16]{2,1,0:T(1,128)S(1)}, f32[6,1,16]{2,1,0:T(1,128)S(1)}, u32[]{:S(2)}, u32[]{:S(2)}) collective-permute-start(f32[6,1,16]{2,1,0:T(1,128)S(1)} %constant_dynamic-update-slice_fusion.5), channel_id=1, source_target_pairs={{0,192},{16,208},{32,224},{48,240},{64,128},{80,144},{96,160},{112... | collective-permute-start | bytes 1160 | tf_op jit(solution)/shard_map/ppermute | solution.py:34
  9.4 0.0 collective-permute-done
  9.5 3.3 %collective-permute-start.1 = (f32[6,32,128]{2,1,0:T(8,128)S(1)}, f32[6,32,128]{2,1,0:T(8,128)S(1)}, u32[]{:S(2)}, u32[]{:S(2)}) collective-permute-start(f32[6,32,128]{2,1,0:T(8,128)S(1)} %pad_maximum_fusion.2), channel_id=1, source_target_pairs={{0,2},{1,3},{2,0},{3,1},{4,6},{5,7},{6,4},{7,5},{8,10},{9,11},{10,... | collective-permute-start | bytes 294920 | tf_op jit(solution)/shard_map/ppermute | solution.py:34
  12.7 0.0 collective-permute-done.4
  12.7 0.1 pad_maximum_fusion.4
  12.8 1.5 %collective-permute-start.5 = (f32[6,1,32]{2,1,0:T(1,128)S(1)}, f32[6,1,32]{2,1,0:T(1,128)S(1)}, u32[]{:S(2)}, u32[]{:S(2)}) collective-permute-start(f32[6,1,32]{2,1,0:T(1,128)S(1)} %pad_maximum_fusion.4), channel_id=1, source_target_pairs={{0,64},{16,80},{32,96},{48,112},{64,0},{80,16},{96,32},{112,48},{1... | collective-permute-start | bytes 2312 | tf_op jit(solution)/shard_map/ppermute | solution.py:34
  14.3 1.4 %collective-permute-done.1 = f32[6,32,128]{2,1,0:T(8,128)S(1)} collective-permute-done((f32[6,32,128]{2,1,0:T(8,128)S(1)}, f32[6,32,128]{2,1,0:T(8,128)S(1)}, u32[]{:S(2)}, u32[]{:S(2)}) %collective-permute-start.1) | collective-permute-done | bytes 98336 | tf_op jit(solution)/shard_map/ppermute | solution.py:34
  15.7 1.9 %collective-permute-start.2 = (f32[6,64,128]{2,1,0:T(8,128)S(1)}, f32[6,64,128]{2,1,0:T(8,128)S(1)}, u32[]{:S(2)}, u32[]{:S(2)}) collective-permute-start(f32[6,64,128]{2,1,0:T(8,128)S(1)} %pad_maximum_fusion.1), channel_id=1, source_target_pairs={{0,4},{1,5},{2,6},{3,7},{4,0},{5,1},{6,2},{7,3},{8,12},{9,13},{10,... | collective-permute-start | bytes 589832 | tf_op jit(solution)/shard_map/ppermute | solution.py:34
  17.6 0.0 collective-permute-done.5
  17.6 0.1 pad_maximum_fusion.5
  17.7 1.1 %collective-permute-start.6 = (f32[6,1,64]{2,1,0:T(1,128)S(1)}, f32[6,1,64]{2,1,0:T(1,128)S(1)}, u32[]{:S(2)}, u32[]{:S(2)}) collective-permute-start(f32[6,1,64]{2,1,0:T(1,128)S(1)} %pad_maximum_fusion.5), channel_id=1, source_target_pairs={{0,32},{16,48},{32,0},{48,16},{64,96},{80,112},{96,64},{112,80},{1... | collective-permute-start | bytes 4616 | tf_op jit(solution)/shard_map/ppermute | solution.py:34
  18.7 2.6 %collective-permute-done.6 = f32[6,1,64]{2,1,0:T(1,128)S(1)} collective-permute-done((f32[6,1,64]{2,1,0:T(1,128)S(1)}, f32[6,1,64]{2,1,0:T(1,128)S(1)}, u32[]{:S(2)}, u32[]{:S(2)}) %collective-permute-start.6) | collective-permute-done | bytes 1568 | tf_op jit(solution)/shard_map/ppermute | solution.py:34
  21.3 0.1 pad_maximum_fusion.6
  21.4 1.7 %collective-permute-start.7 = (f32[6,1,128]{2,1,0:T(1,128)S(1)}, f32[6,1,128]{2,1,0:T(1,128)S(1)}, u32[]{:S(2)}, u32[]{:S(2)}) collective-permute-start(f32[6,1,128]{2,1,0:T(1,128)S(1)} %pad_maximum_fusion.6), channel_id=1, source_target_pairs={{0,16},{16,0},{32,48},{48,32},{64,80},{80,64},{96,112},{112,96},{1... | collective-permute-start | bytes 9224 | tf_op jit(solution)/shard_map/ppermute | solution.py:34
  23.0 3.0 %kept_tiles.1.list_ref = s32[548]{0:T(1024)} custom-call(s32[2,2,128]{2,1,0:T(2,128)} %bitcast.19), custom_call_target="tpu_custom_call" | custom-call | tf_op jit(solution)/shard_map/kept_tiles/pallas_call | solution.py:139
  26.1 0.0 collective-permute-done.2
  26.1 0.1 collective-permute-start.3
  26.3 0.0 collective-permute-done.7
  26.3 0.1 concatenate.45
  26.4 1.5 %collective-permute-done.3 = f32[6,128,128]{2,1,0:T(8,128)S(1)} collective-permute-done((f32[6,128,128]{2,1,0:T(8,128)S(1)}, f32[6,128,128]{2,1,0:T(8,128)S(1)}, u32[]{:S(2)}, u32[]{:S(2)}) %collective-permute-start.3) | collective-permute-done | bytes 393248 | tf_op jit(solution)/shard_map/ppermute | solution.py:34
  28.0 0.1 pad.4.nod_ref
  28.0 0.3 broadcast_in_dim.11.ctl_ref
  28.3 0.0 copy-start
  28.3 0.7 copy-done
  29.0 18.6 %pairs.2 = (f32[3,128,128]{2,1,0:T(8,128)S(1)}, f32[6,1,256]{2,1,0:T(1,128)S(1)}) custom-call(s32[548]{0:T(1024)S(1)} %copy-done, f32[6,264,128]{2,1,0:T(8,128)S(1)} %pad.4.nod_ref, f32[6,256,128]{2,1,0:T(8,128)S(1)} %broadcast_in_dim.11.ctl_ref, f32[6,1,256]{2,1,0:T(1,128)S(1)} %broadcast_in_dim.12.before_ref), custom_call_target="tpu_custom_call" | custom-call | flops 20971520000 | bytes 67108864 | tf_op jit(solution)/shard_map/pairs/pallas_call | solution.py:155
  47.6 0.1 collective-permute-start.8
  47.7 17.5 %pairs.3 = (f32[3,128,128]{2,1,0:T(8,128)S(1)}, f32[6,1,256]{2,1,0:T(1,128)S(1)}) custom-call(s32[548]{0:T(1024)S(1)} %copy-done, f32[6,264,128]{2,1,0:T(8,128)S(1)} %pad.4.nod_ref, f32[6,256,128]{2,1,0:T(8,128)S(1)} %broadcast_in_dim.11.ctl_ref, f32[6,1,256]{2,1,0:T(1,128)S(1)} %get-tuple-element.23.before_ref), custom_call_target="tpu_custom_call" | custom-call | flops 20971520000 | bytes 67108864 | tf_op jit(solution)/shard_map/pairs/pallas_call | solution.py:155
  65.1 0.0 collective-permute-done.8
  65.2 1.2 %collective-permute-start.9 = (f32[6,1,128]{2,1,0:T(1,128)S(1)}, f32[6,1,128]{2,1,0:T(1,128)S(1)}, u32[]{:S(2)}, u32[]{:S(2)}) collective-permute-start(f32[6,1,128]{2,1,0:T(1,128)S(1)} %slice.49), channel_id=1, source_target_pairs={{0,16},{16,0},{32,48},{48,32},{64,80},{80,64},{96,112},{112,96},{1... | collective-permute-start | bytes 9224 | tf_op jit(solution)/shard_map/ppermute | solution.py:34
  66.4 2.5 %collective-permute-start.11 = (f32[3,64,128]{2,1,0:T(8,128)S(1)}, f32[3,64,128]{2,1,0:T(8,128)S(1)}, u32[]{:S(2)}, u32[]{:S(2)}) collective-permute-start(f32[3,64,128]{2,1,0:T(8,128)S(1)} %get-tuple-element.41), channel_id=1, source_target_pairs={{0,2},{1,3},{2,0},{3,1},{4,6},{5,7},{6,4},{7,5},{8,10},{9,11},{10,... | collective-permute-start | bytes 294920 | tf_op jit(solution)/shard_map/ppermute | solution.py:34
  68.9 0.0 collective-permute-done.9
  68.9 0.1 slice.65
  69.0 2.5 %collective-permute-start.10 = (f32[6,1,64]{2,1,0:T(1,128)S(1)}, f32[6,1,64]{2,1,0:T(1,128)S(1)}, u32[]{:S(2)}, u32[]{:S(2)}) collective-permute-start(f32[6,1,64]{2,1,0:T(1,128)S(1)} %slice.65), channel_id=1, source_target_pairs={{0,32},{16,48},{32,0},{48,16},{64,96},{80,112},{96,64},{112,80},{1... | collective-permute-start | bytes 4616 | tf_op jit(solution)/shard_map/ppermute | solution.py:34
  71.5 1.6 %collective-permute-done.10 = f32[6,1,64]{2,1,0:T(1,128)S(1)} collective-permute-done((f32[6,1,64]{2,1,0:T(1,128)S(1)}, f32[6,1,64]{2,1,0:T(1,128)S(1)}, u32[]{:S(2)}, u32[]{:S(2)}) %collective-permute-start.10) | collective-permute-done | bytes 1568 | tf_op jit(solution)/shard_map/ppermute | solution.py:34
  73.0 0.0 collective-permute-done.11
  73.1 3.9 %collective-permute-start.13 = (f32[3,32,128]{2,1,0:T(8,128)S(1)}, f32[3,32,128]{2,1,0:T(8,128)S(1)}, u32[]{:S(2)}, u32[]{:S(2)}) collective-permute-start(f32[3,32,128]{2,1,0:T(8,128)S(1)} %get-tuple-element.43), channel_id=1, source_target_pairs={{0,4},{1,5},{2,6},{3,7},{4,0},{5,1},{6,2},{7,3},{8,12},{9,13},{10,... | collective-permute-start | bytes 147464 | tf_op jit(solution)/shard_map/ppermute | solution.py:34
  77.0 0.1 slice.68
  77.1 0.0 collective-permute-start.12
  77.1 4.5 %collective-permute-done.12 = f32[6,1,32]{2,1,0:T(1,128)S(1)} collective-permute-done((f32[6,1,32]{2,1,0:T(1,128)S(1)}, f32[6,1,32]{2,1,0:T(1,128)S(1)}, u32[]{:S(2)}, u32[]{:S(2)}) %collective-permute-start.12) | collective-permute-done | bytes 800 | tf_op jit(solution)/shard_map/ppermute | solution.py:34
  81.6 0.0 collective-permute-done.13
  81.6 0.1 slice.75
  81.7 2.2 %collective-permute-start.15 = (f32[6,1,16]{2,1,0:T(1,128)S(1)}, f32[6,1,16]{2,1,0:T(1,128)S(1)}, u32[]{:S(2)}, u32[]{:S(2)}) collective-permute-start(f32[6,1,16]{2,1,0:T(1,128)S(1)} %slice.75), channel_id=1, source_target_pairs={{0,192},{16,208},{32,224},{48,240},{64,128},{80,144},{96,160},{112... | collective-permute-start | bytes 1160 | tf_op jit(solution)/shard_map/ppermute | solution.py:34
  83.9 0.1 collective-permute-start.14
  84.0 3.4 %collective-permute-done.15 = f32[6,1,16]{2,1,0:T(1,128)S(1)} collective-permute-done((f32[6,1,16]{2,1,0:T(1,128)S(1)}, f32[6,1,16]{2,1,0:T(1,128)S(1)}, u32[]{:S(2)}, u32[]{:S(2)}) %collective-permute-start.15) | collective-permute-done | bytes 416 | tf_op jit(solution)/shard_map/ppermute | solution.py:34
  87.4 0.6 slice_multiply_fusion
  88.0 0.0 collective-permute-done.14
  88.0 0.6 fusion
  (23 shorter events, 0.2 us)
Async XLA Ops:
  1.4 1.6 %copy-start.1 = (f32[3,1,16]{2,1,0:T(1,128)S(1)}, f32[3,1,16]{2,1,0:T(1,128)}, u32[]{:S(2)}) copy-start(f32[3,1,16]{2,1,0:T(1,128)} %param.7) | copy-start | bytes 580
  1.4 1.6 %copy-start.2 = (f32[3,1,16]{2,1,0:T(1,128)S(1)}, f32[3,1,16]{2,1,0:T(1,128)}, u32[]{:S(2)}) copy-start(f32[3,1,16]{2,1,0:T(1,128)} %param.8) | copy-start | bytes 580
  1.5 8.0 %collective-permute-start = (f32[6,16,128]{2,1,0:T(8,128)S(1)}, f32[6,16,128]{2,1,0:T(8,128)S(1)}, u32[]{:S(2)}, u32[]{:S(2)}) collective-permute-start(f32[6,16,128]{2,1,0:T(8,128)S(1)} %bitcast.12), channel_id=1, source_target_pairs={{0,12},{1,13},{2,14},{3,15},{4,8},{5,9},{6,10},{7,11},{8,4},{9,5},... | collective-permute-start | bytes 147464 | tf_op jit(solution)/shard_map/ppermute | solution.py:34
  3.1 9.7 %collective-permute-start.4 = (f32[6,1,16]{2,1,0:T(1,128)S(1)}, f32[6,1,16]{2,1,0:T(1,128)S(1)}, u32[]{:S(2)}, u32[]{:S(2)}) collective-permute-start(f32[6,1,16]{2,1,0:T(1,128)S(1)} %constant_dynamic-update-slice_fusion.5), channel_id=1, source_target_pairs={{0,192},{16,208},{32,224},{48,240},{64,128},{80,144},{96,160},{112... | collective-permute-start | bytes 1160 | tf_op jit(solution)/shard_map/ppermute | solution.py:34
  9.5 6.2 %collective-permute-start.1 = (f32[6,32,128]{2,1,0:T(8,128)S(1)}, f32[6,32,128]{2,1,0:T(8,128)S(1)}, u32[]{:S(2)}, u32[]{:S(2)}) collective-permute-start(f32[6,32,128]{2,1,0:T(8,128)S(1)} %pad_maximum_fusion.2), channel_id=1, source_target_pairs={{0,2},{1,3},{2,0},{3,1},{4,6},{5,7},{6,4},{7,5},{8,10},{9,11},{10,... | collective-permute-start | bytes 294920 | tf_op jit(solution)/shard_map/ppermute | solution.py:34
  12.8 4.8 %collective-permute-start.5 = (f32[6,1,32]{2,1,0:T(1,128)S(1)}, f32[6,1,32]{2,1,0:T(1,128)S(1)}, u32[]{:S(2)}, u32[]{:S(2)}) collective-permute-start(f32[6,1,32]{2,1,0:T(1,128)S(1)} %pad_maximum_fusion.4), channel_id=1, source_target_pairs={{0,64},{16,80},{32,96},{48,112},{64,0},{80,16},{96,32},{112,48},{1... | collective-permute-start | bytes 2312 | tf_op jit(solution)/shard_map/ppermute | solution.py:34
  15.7 10.4 %collective-permute-start.2 = (f32[6,64,128]{2,1,0:T(8,128)S(1)}, f32[6,64,128]{2,1,0:T(8,128)S(1)}, u32[]{:S(2)}, u32[]{:S(2)}) collective-permute-start(f32[6,64,128]{2,1,0:T(8,128)S(1)} %pad_maximum_fusion.1), channel_id=1, source_target_pairs={{0,4},{1,5},{2,6},{3,7},{4,0},{5,1},{6,2},{7,3},{8,12},{9,13},{10,... | collective-permute-start | bytes 589832 | tf_op jit(solution)/shard_map/ppermute | solution.py:34
  17.7 3.6 %collective-permute-start.6 = (f32[6,1,64]{2,1,0:T(1,128)S(1)}, f32[6,1,64]{2,1,0:T(1,128)S(1)}, u32[]{:S(2)}, u32[]{:S(2)}) collective-permute-start(f32[6,1,64]{2,1,0:T(1,128)S(1)} %pad_maximum_fusion.5), channel_id=1, source_target_pairs={{0,32},{16,48},{32,0},{48,16},{64,96},{80,112},{96,64},{112,80},{1... | collective-permute-start | bytes 4616 | tf_op jit(solution)/shard_map/ppermute | solution.py:34
  21.4 4.9 %collective-permute-start.7 = (f32[6,1,128]{2,1,0:T(1,128)S(1)}, f32[6,1,128]{2,1,0:T(1,128)S(1)}, u32[]{:S(2)}, u32[]{:S(2)}) collective-permute-start(f32[6,1,128]{2,1,0:T(1,128)S(1)} %pad_maximum_fusion.6), channel_id=1, source_target_pairs={{0,16},{16,0},{32,48},{48,32},{64,80},{80,64},{96,112},{112,96},{1... | collective-permute-start | bytes 9224 | tf_op jit(solution)/shard_map/ppermute | solution.py:34
  26.1 1.8 %collective-permute-start.3 = (f32[6,128,128]{2,1,0:T(8,128)S(1)}, f32[6,128,128]{2,1,0:T(8,128)S(1)}, u32[]{:S(2)}, u32[]{:S(2)}) collective-permute-start(f32[6,128,128]{2,1,0:T(8,128)S(1)} %pad_maximum_fusion), channel_id=1, source_target_pairs={{0,1},{1,0},{2,3},{3,2},{4,5},{5,4},{6,7},{7,6},{8,9},{9,8},{10,11... | collective-permute-start | bytes 1179656 | tf_op jit(solution)/shard_map/ppermute | solution.py:34
  28.3 0.7 copy-start
  47.6 17.6 %collective-permute-start.8 = (f32[3,128,128]{2,1,0:T(8,128)S(1)}, f32[3,128,128]{2,1,0:T(8,128)S(1)}, u32[]{:S(2)}, u32[]{:S(2)}) collective-permute-start(f32[3,128,128]{2,1,0:T(8,128)S(1)} %get-tuple-element.25), channel_id=1, source_target_pairs={{0,12},{1,13},{2,14},{3,15},{4,8},{5,9},{6,10},{7,11},{8,4},{9,5},... | collective-permute-start | bytes 589832 | tf_op jit(solution)/shard_map/ppermute | solution.py:34
  65.2 3.7 %collective-permute-start.9 = (f32[6,1,128]{2,1,0:T(1,128)S(1)}, f32[6,1,128]{2,1,0:T(1,128)S(1)}, u32[]{:S(2)}, u32[]{:S(2)}) collective-permute-start(f32[6,1,128]{2,1,0:T(1,128)S(1)} %slice.49), channel_id=1, source_target_pairs={{0,16},{16,0},{32,48},{48,32},{64,80},{80,64},{96,112},{112,96},{1... | collective-permute-start | bytes 9224 | tf_op jit(solution)/shard_map/ppermute | solution.py:34
  66.4 6.6 %collective-permute-start.11 = (f32[3,64,128]{2,1,0:T(8,128)S(1)}, f32[3,64,128]{2,1,0:T(8,128)S(1)}, u32[]{:S(2)}, u32[]{:S(2)}) collective-permute-start(f32[3,64,128]{2,1,0:T(8,128)S(1)} %get-tuple-element.41), channel_id=1, source_target_pairs={{0,2},{1,3},{2,0},{3,1},{4,6},{5,7},{6,4},{7,5},{8,10},{9,11},{10,... | collective-permute-start | bytes 294920 | tf_op jit(solution)/shard_map/ppermute | solution.py:34
  69.0 4.1 %collective-permute-start.10 = (f32[6,1,64]{2,1,0:T(1,128)S(1)}, f32[6,1,64]{2,1,0:T(1,128)S(1)}, u32[]{:S(2)}, u32[]{:S(2)}) collective-permute-start(f32[6,1,64]{2,1,0:T(1,128)S(1)} %slice.65), channel_id=1, source_target_pairs={{0,32},{16,48},{32,0},{48,16},{64,96},{80,112},{96,64},{112,80},{1... | collective-permute-start | bytes 4616 | tf_op jit(solution)/shard_map/ppermute | solution.py:34
  73.1 8.5 %collective-permute-start.13 = (f32[3,32,128]{2,1,0:T(8,128)S(1)}, f32[3,32,128]{2,1,0:T(8,128)S(1)}, u32[]{:S(2)}, u32[]{:S(2)}) collective-permute-start(f32[3,32,128]{2,1,0:T(8,128)S(1)} %get-tuple-element.43), channel_id=1, source_target_pairs={{0,4},{1,5},{2,6},{3,7},{4,0},{5,1},{6,2},{7,3},{8,12},{9,13},{10,... | collective-permute-start | bytes 147464 | tf_op jit(solution)/shard_map/ppermute | solution.py:34
  77.1 4.5 %collective-permute-start.12 = (f32[6,1,32]{2,1,0:T(1,128)S(1)}, f32[6,1,32]{2,1,0:T(1,128)S(1)}, u32[]{:S(2)}, u32[]{:S(2)}) collective-permute-start(f32[6,1,32]{2,1,0:T(1,128)S(1)} %slice.68), channel_id=1, source_target_pairs={{0,64},{16,80},{32,96},{48,112},{64,0},{80,16},{96,32},{112,48},{1... | collective-permute-start | bytes 2312 | tf_op jit(solution)/shard_map/ppermute | solution.py:34
  81.7 5.7 %collective-permute-start.15 = (f32[6,1,16]{2,1,0:T(1,128)S(1)}, f32[6,1,16]{2,1,0:T(1,128)S(1)}, u32[]{:S(2)}, u32[]{:S(2)}) collective-permute-start(f32[6,1,16]{2,1,0:T(1,128)S(1)} %slice.75), channel_id=1, source_target_pairs={{0,192},{16,208},{32,224},{48,240},{64,128},{80,144},{96,160},{112... | collective-permute-start | bytes 1160 | tf_op jit(solution)/shard_map/ppermute | solution.py:34
  83.9 4.1 %collective-permute-start.14 = (f32[3,16,128]{2,1,0:T(8,128)S(1)}, f32[3,16,128]{2,1,0:T(8,128)S(1)}, u32[]{:S(2)}, u32[]{:S(2)}) collective-permute-start(f32[3,16,128]{2,1,0:T(8,128)S(1)} %slice.72), channel_id=1, source_target_pairs={{0,1},{1,0},{2,3},{3,2},{4,5},{5,4},{6,7},{7,6},{8,9},{9,8},{10,11... | collective-permute-start | bytes 73736 | tf_op jit(solution)/shard_map/ppermute | solution.py:34
